TPU v7x, 256 devices: a whole 4x4x8 slice. The times are simulated.
256 devices in a mesh: segment: 2 (over z_hi), mp: 16 (over y, x), dp: 8 (over z_lo, core).
Axes of the slice: x: 4, y: 4, z: 8 (z_hi: 2, z_lo: 4; z = z_hi * 4 + z_lo), core: 2. Of those that a mesh axis runs over, the one named last changes fastest.
Arguments:
- hidden: bfloat16 [32768, 3584], P(('segment', 'mp', 'dp')), may hold values from -6 to 6
- chat_owner_index: int32 [8192], P(('segment', 'mp', 'dp')), may hold values from 0 to 15, as said below
- thinker_to_talker_weight: bfloat16 [3584, 896], P('dp'), may hold values from -0.09375 to 0.09375
- attention_norm_gain: bfloat16 [896], replicated, may hold values from 0.099609375 to 1.8984375
- talker_query_weight: bfloat16 [896, 768], replicated, may hold values from -0.1875 to 0.1875
- talker_key_weight: bfloat16 [896, 256], replicated, may hold values from -0.1875 to 0.1875
- talker_value_weight: bfloat16 [896, 256], replicated, may hold values from -0.1875 to 0.1875
- talker_key_value_cache: bfloat16 [16384, 2, 48, 256], P(('segment', 'mp', 'dp')), may hold values from -360 to 360
- cache_fill_length: int32 [16384], P(('segment', 'mp', 'dp')), may hold values from 1 to 48
- noisy_flow_rows: bfloat16 [32768, 1024], P(('segment', 'mp', 'dp')), may hold values from -6 to 6
- flow_expand_weight: bfloat16 [2048, 1792], P('mp'), may hold values from -0.125 to 0.125
- flow_reduce_weight: bfloat16 [2048, 1024], P('mp'), may hold values from -0.125 to 0.125
Outputs:
- flowed: bfloat16 [32768, 1024], P(('segment', 'mp', 'dp'))
Inputs may be any that keep to these rules, and one draw needn't show every extreme that they name: `chat_owner_index`: every owner is among the 16 mp devices of the source's own segment and dp index; a device sends at most 4 conversations to one owner, and in each segment and dp group one owner receives exactly 4 from every device of the group.
All inputs are finite; a program needn't handle non-finite values.
Results may differ from a plain program's by a relative error of at most 0.012.
Values may be sent and summed in bfloat16 or wider, within the bound.
A program may use at most 128 MiB of HBM per device.

v0:
```python
import jax
import jax.numpy as jnp
from jax import lax
from jax.sharding import PartitionSpec as P

HEAD_SIZE = 128
DECODE_STEPS = 4


def partner(x, axis, apart):
    return lax.ppermute(x, axis, [(i, i ^ 1 << apart) for i in range(lax.axis_size(axis))])


def rms_scale(values):
    return values * lax.rsqrt(jnp.mean(values * values, axis=-1, keepdims=True) + 1e-06)


def owner_ranks(owners, owner_count):
    onehot = (owners[:, None] == jnp.arange(owner_count, dtype=jnp.int32)[None, :]).astype(
        jnp.int32
    )
    before = jnp.cumsum(onehot, axis=0) - onehot
    return jnp.sum(before * onehot, axis=1)


def attend(query_rows, new_key_rows, new_value_rows, cached, lengths):
    conv_count = query_rows.shape[0]
    step_count = query_rows.shape[1]
    kv_heads = new_key_rows.shape[2] // HEAD_SIZE
    groups = query_rows.shape[2] // (HEAD_SIZE * kv_heads)
    cache_span = cached.shape[2]
    query_heads = query_rows.reshape(conv_count, step_count, kv_heads, groups, HEAD_SIZE).astype(
        jnp.float32
    )
    key_fresh = new_key_rows.reshape(conv_count, step_count, kv_heads, HEAD_SIZE).astype(
        jnp.float32
    )
    value_fresh = new_value_rows.reshape(conv_count, step_count, kv_heads, HEAD_SIZE).astype(
        jnp.float32
    )
    key_cached = (
        cached[:, 0].reshape(conv_count, cache_span, kv_heads, HEAD_SIZE).astype(jnp.float32)
    )
    value_cached = (
        cached[:, 1].reshape(conv_count, cache_span, kv_heads, HEAD_SIZE).astype(jnp.float32)
    )
    factor = HEAD_SIZE ** (-0.5)
    score_cached = jnp.einsum("stkgd,sckd->stkgc", query_heads, key_cached) * factor
    score_fresh = jnp.einsum("stkgd,sukd->stkgu", query_heads, key_fresh) * factor
    cache_live = jnp.arange(cache_span, dtype=jnp.int32)[None, :] < lengths[:, None]
    causal = jnp.arange(step_count)[None, :] <= jnp.arange(step_count)[:, None]
    score_cached = jnp.where(cache_live[:, None, None, None, :], score_cached, -jnp.inf)
    score_fresh = jnp.where(causal[None, :, None, None, :], score_fresh, -jnp.inf)
    peak_score = jnp.maximum(jnp.max(score_cached, axis=-1), jnp.max(score_fresh, axis=-1))
    prob_cached = jnp.exp(score_cached - peak_score[..., None])
    prob_fresh = jnp.exp(score_fresh - peak_score[..., None])
    weight_sum = jnp.sum(prob_cached, axis=-1) + jnp.sum(prob_fresh, axis=-1)
    weight_cached = (prob_cached / weight_sum[..., None]).astype(jnp.bfloat16)
    weight_fresh = (prob_fresh / weight_sum[..., None]).astype(jnp.bfloat16)
    attended = jnp.einsum("stkgc,sckd->stkgd", weight_cached.astype(jnp.float32), value_cached)
    attended = attended + jnp.einsum(
        "stkgu,sukd->stkgd", weight_fresh.astype(jnp.float32), value_fresh
    )
    return attended.reshape(conv_count, step_count, kv_heads * groups * HEAD_SIZE).astype(
        jnp.bfloat16
    )


def widened_rows(input_rows, expand_part):
    widened_hidden = lax.dot_general(
        input_rows, expand_part, (((1,), (1,)), ((), ())), preferred_element_type=jnp.float32
    )
    return jax.nn.gelu(widened_hidden).astype(jnp.bfloat16)


def shards(
    hidden,
    chat_owner_index,
    thinker_to_talker_weight,
    attention_norm_gain,
    talker_query_weight,
    talker_key_weight,
    talker_value_weight,
    talker_key_value_cache,
    cache_fill_length,
    noisy_flow_rows,
    flow_expand_weight,
    flow_reduce_weight,
):
    mp_count = lax.axis_size("mp")
    conv_count = chat_owner_index.shape[0]
    capacity = 2 * conv_count // mp_count
    owner_rank = owner_ranks(chat_owner_index, mp_count)
    target = chat_owner_index * capacity + owner_rank
    row_width = hidden.shape[1]
    grouped = hidden.reshape(conv_count, DECODE_STEPS, row_width)
    packed = (
        jnp.zeros((mp_count * capacity, DECODE_STEPS, row_width), hidden.dtype)
        .at[target]
        .set(grouped)
    )
    outgoing = packed.reshape(mp_count, capacity * DECODE_STEPS, row_width)
    arrived = lax.all_to_all(outgoing, "mp", split_axis=0, concat_axis=0, tiled=True)
    owner_rows = arrived.reshape(mp_count * capacity * DECODE_STEPS, arrived.shape[2])
    projected = jnp.dot(
        owner_rows,
        lax.all_gather(thinker_to_talker_weight, "dp", axis=0, tiled=True),
        preferred_element_type=jnp.float32,
    ).astype(jnp.bfloat16)
    normed = (
        rms_scale(projected.astype(jnp.float32)) * attention_norm_gain.astype(jnp.float32)
    ).astype(jnp.bfloat16)
    query_rows = jnp.dot(normed, talker_query_weight, preferred_element_type=jnp.float32).astype(
        jnp.bfloat16
    )
    new_key_rows = jnp.dot(normed, talker_key_weight, preferred_element_type=jnp.float32).astype(
        jnp.bfloat16
    )
    new_value_rows = jnp.dot(
        normed, talker_value_weight, preferred_element_type=jnp.float32
    ).astype(jnp.bfloat16)
    slot_count = mp_count * capacity
    attended = attend(
        query_rows.reshape(slot_count, DECODE_STEPS, query_rows.shape[1]),
        new_key_rows.reshape(slot_count, DECODE_STEPS, new_key_rows.shape[1]),
        new_value_rows.reshape(slot_count, DECODE_STEPS, new_value_rows.shape[1]),
        talker_key_value_cache,
        cache_fill_length,
    )
    out_width = attended.shape[2]
    returned = lax.all_to_all(
        attended.reshape(mp_count, capacity * DECODE_STEPS, out_width),
        "mp",
        split_axis=0,
        concat_axis=0,
        tiled=True,
    )
    own_rows = returned.reshape(slot_count, DECODE_STEPS, out_width)[target].reshape(
        conv_count * DECODE_STEPS, out_width
    )
    paired_device = partner(own_rows, "segment", 0)
    flow_input_rows = jnp.concatenate([noisy_flow_rows, paired_device], axis=1)
    feedforward_hidden = widened_rows(
        flow_input_rows, lax.all_gather(flow_expand_weight, "mp", axis=0, tiled=True)
    )
    flow_velocity = jnp.dot(
        feedforward_hidden,
        lax.all_gather(flow_reduce_weight, "mp", axis=0, tiled=True),
        preferred_element_type=jnp.float32,
    )
    return (noisy_flow_rows.astype(jnp.float32) + 0.5 * flow_velocity).astype(jnp.bfloat16)


def solution(mesh):
    placed = (
        P(("segment", "mp", "dp"), None),
        P(("segment", "mp", "dp")),
        P("dp", None),
        P(),
        P(),
        P(),
        P(),
        P(("segment", "mp", "dp"), None, None, None),
        P(("segment", "mp", "dp")),
        P(("segment", "mp", "dp"), None),
        P("mp", None),
        P("mp", None),
    )
    return jax.shard_map(
        shards,
        mesh=mesh,
        in_specs=placed,
        out_specs=P(("segment", "mp", "dp"), None),
        check_vma=False,
    )
```

profile of v0, /device:TPU:1, one launch (start us, length us, event | category | flops | bytes accessed | tf_op | source)
XLA Modules:
  0.0 234.4 jit_solution(10375090114438376057)
XLA Ops:
  6.5 0.0 copy-start
  6.5 0.0 all-gather.4.cloned.1.call-start
  6.5 0.7 all-gather.4.cloned.1.call-update
  7.3 0.0 all-gather.8.cloned.1.call-start
  7.3 0.7 all-gather.8.cloned.1.call-update
  8.0 0.0 all-gather.6.cloned.1.call-start
  8.1 0.7 all-gather.6.cloned.1.call-update
  8.7 0.0 copy-done.1
  8.8 1.2 reshape.85
  9.9 0.0 copy-done.5
  9.9 0.1 fusion.58
  10.0 0.1 reduce_window_sum.11
  10.1 0.2 select_reduce_fusion
  10.3 0.5 broadcast_in_dim.29
  10.8 3.6 %scatter_fusion = bf16[64,4,3584]{2,1,0:T(4,128)(2,1)S(1)} fusion(bf16[64,4,3584]{2,1,0:T(4,128)(2,1)S(1)} %broadcast_in_dim.29, s32[32]{0:T(128)S(1)} %compare_select_fusion, bf16[32,4,3584]{2,1,0:T(4,128)(2,1)} %reshape.85), kind=kCustom, calls=%fused_computation.1 | custom fusion | bytes 2752640 | tf_op jit(solution)/shard_map/scatter | solution.py:100
  14.3 1.5 reshape.69
  15.8 7.8 %all-to-all-start = ((bf16[16,16,3584]{2,1,0:T(8,128)(2,1)}), bf16[16,16,3584]{2,1,0:T(8,128)(2,1)}, u32[]{:S(2)}, u32[]{:S(2)}) async-start(bf16[16,16,3584]{2,1,0:T(8,128)(2,1)} %reshape.69), calls=%async_computation | async-start | bytes 3670016 | tf_op jit(solution)/shard_map/all_to_all | solution.py:103
  23.6 0.0 copy-done.4
  23.6 3.5 %fusion.65 = (bf16[64,1,48,256]{3,2,1,0:T(8,128)(2,1)S(1)}, bf16[64,1,48,256]{3,2,1,0:T(8,128)(2,1)}) fusion(bf16[64,2,48,256]{3,2,1,0:T(8,128)(2,1)} %param.19), kind=kLoop, calls=%fused_computation.68 | loop fusion | bytes 6291456 | tf_op jit(solution)/shard_map/slice | solution.py:45
  27.1 3.5 %reshape_squeeze.6 = bf16[64,48,2,128]{3,2,1,0:T(2,128)(2,1)} reshape(bf16[64,1,48,256]{3,2,1,0:T(8,128)(2,1)} %get-tuple-element.6) | data formatting | bytes 3145728 | tf_op jit(solution)/shard_map/reshape;squeeze | solution.py:42
  30.7 1.9 reshape_squeeze.7
  32.5 0.0 copy-done.6
  32.5 0.1 iota_compare_fusion
  32.6 17.8 %all-to-all-done = bf16[16,16,3584]{2,1,0:T(8,128)(2,1)} async-done(((bf16[16,16,3584]{2,1,0:T(8,128)(2,1)}), bf16[16,16,3584]{2,1,0:T(8,128)(2,1)}, u32[]{:S(2)}, u32[]{:S(2)}) %all-to-all-start) | async-done | bytes 1835040 | tf_op jit(solution)/shard_map/all_to_all | solution.py:103
  50.4 35.8 %all-gather.4.cloned.1.call-done = bf16[3584,896]{1,0:T(8,128)(2,1)} async-done(((bf16[448,896]{1,0:T(8,128)(2,1)}), bf16[3584,896]{1,0:T(8,128)(2,1)}) %all-gather.4.cloned.1.call-update) | async-done | bytes 6422544 | tf_op jit(solution)/shard_map/all_gather | solution.py:107
  86.2 5.5 %multiply_reduce_fusion = (f32[256]{0:T(256)S(1)}, f32[256,896]{1,0:T(8,128)S(1)}) fusion(bf16[256,3584]{1,0:T(8,128)(2,1)} %bitcast, bf16[3584,896]{1,0:T(8,128)(2,1)} %all-gather.4.cloned.1.call-done), kind=kOutput, calls=%fused_computation.31 | convolution fusion | flops 1645084416 | bytes 9176064 | tf_op jit(solution)/shard_map/dot_general | solution.py:105
  91.7 0.2 multiply_convert_fusion
  91.9 0.0 copy-done
  91.9 0.0 copy-start.3
  91.9 0.6 convolution_convert_fusion.1
  92.5 0.2 reshape_reshape.9
  92.7 0.3 copy-done.3
  92.9 0.3 convolution_convert_fusion.3
  93.3 0.4 fusion.35
  93.7 0.7 copy.52
  94.5 0.1 fusion.57
  94.6 0.2 copy.53
  94.8 2.5 %fusion.66 = (f32[64,4,2,3]{1,3,2,0:T(4,128)S(1)}, f32[64,4,2,3,48]{4,1,3,2,0:T(4,128)S(1)}) fusion(bf16[64,48,2,128,1]{3,2,1,0,4:T(2,128)(2,1)} %bitcast.39, bf16[64,4,2,3,128]{4,3,2,1,0:T(4,128)(2,1)S(1)} %reshape_reshape.9, pred[64,48]{1,0:T(8,128)(4,1)S(1)} %iota_compare_fusion), kind=kOutput, calls=%fused_computation.69 | convolution fusion | flops 19094016 | bytes 2270208 | tf_op jit(solution)/shard_map/stkgd,sckd->stkgc/dot_general | solution.py:48
  97.3 0.1 max.7
  97.4 0.1 copy.54
  97.5 0.1 fusion.56
  97.7 0.2 copy.55
  97.9 0.4 copy-done.2
  98.2 1.0 fusion.33
  99.3 0.1 add.44
  99.4 0.1 copy.57
  99.5 0.1 divide_convert_fusion.2
  99.6 0.3 copy.59
  99.9 1.3 convolution_convert_fusion.2
  101.3 0.5 convolution_bitcast_fusion
  101.8 2.9 %fusion.20 = bf16[64,4,2,3,128]{4,1,3,2,0:T(4,128)(2,1)S(1)} fusion(f32[64,4,2,3,128]{4,1,3,2,0:T(4,128)S(1)} %convolution_bitcast_fusion, bf16[64,48,2,128,1]{3,2,1,0,4:T(2,128)(2,1)} %bitcast.38, f32[64,4,2,3,48]{4,1,3,2,0:T(4,128)} %copy-done.2, f32[64,4,2,3]{1,3,2,0:T(4,128)S(1)} %add.44, f32[64,4,2,3]{1,3,2,0:T(4,128)S(1)} %max.7), kind=kOutput, calls=%fused_computation.16 | convolution fusion | flops 19488768 | bytes 3059712 | tf_op jit(solution)/shard_map/stkgc,sckd->stkgd/dot_general | solution.py:60
  104.8 0.2 copy.60
  105.0 0.0 copy-start.7
  105.0 1.1 convert_element_type.65
  106.1 6.5 %all-to-all-start.1 = ((bf16[16,16,768]{2,1,0:T(8,128)(2,1)}), bf16[16,16,768]{2,1,0:T(8,128)(2,1)S(1)}, u32[]{:S(2)}, u32[]{:S(2)}) async-start(bf16[16,16,768]{2,1,0:T(8,128)(2,1)} %convert_element_type.65), calls=%async_computation.1 | async-start | bytes 786432 | tf_op jit(solution)/shard_map/all_to_all | solution.py:131
  112.6 8.4 %all-to-all-done.1 = bf16[16,16,768]{2,1,0:T(8,128)(2,1)S(1)} async-done(((bf16[16,16,768]{2,1,0:T(8,128)(2,1)}), bf16[16,16,768]{2,1,0:T(8,128)(2,1)S(1)}, u32[]{:S(2)}, u32[]{:S(2)}) %all-to-all-start.1) | async-done | bytes 393248 | tf_op jit(solution)/shard_map/all_to_all | solution.py:131
  121.1 0.1 reshape.71
  121.2 0.7 gather_fusion
  121.9 0.1 reshape.72
  122.0 6.7 %collective-permute-start = (bf16[128,768]{1,0:T(8,128)(2,1)S(1)}, bf16[128,768]{1,0:T(8,128)(2,1)S(1)}, u32[]{:S(2)}, u32[]{:S(2)}) collective-permute-start(bf16[128,768]{1,0:T(8,128)(2,1)S(1)} %reshape.72), channel_id=1, source_target_pairs={{0,128},{128,0},{1,129},{129,1},{2,130},{130,2},{3,131},{131,3},{4... | collective-permute-start | bytes 589832 | tf_op jit(solution)/shard_map/ppermute | solution.py:11
  128.6 17.8 %all-gather.8.cloned.1.call-done = bf16[2048,1024]{1,0:T(8,128)(2,1)} async-done(((bf16[128,1024]{1,0:T(8,128)(2,1)}), bf16[2048,1024]{1,0:T(8,128)(2,1)}) %all-gather.8.cloned.1.call-update) | async-done | bytes 4194320 | tf_op jit(solution)/shard_map/all_gather | solution.py:148
  146.4 0.0 collective-permute-done
  146.4 73.4 %all-gather.6.cloned.1.call-done = bf16[2048,1792]{1,0:T(8,128)(2,1)} async-done(((bf16[128,1792]{1,0:T(8,128)(2,1)}), bf16[2048,1792]{1,0:T(8,128)(2,1)}) %all-gather.6.cloned.1.call-update) | async-done | bytes 7340048 | tf_op jit(solution)/shard_map/all_gather | solution.py:144
  219.8 8.1 %fusion.24 = bf16[128,1024]{1,0:T(8,128)(2,1)} fusion(bf16[2048,1024]{1,0:T(8,128)(2,1)} %all-gather.8.cloned.1.call-done, bf16[128,1024]{1,0:T(8,128)(2,1)S(1)} %copy-done.7, bf16[2048,1792]{1,0:T(8,128)(2,1)} %all-gather.6.cloned.1.call-done, bf16[128,768]{1,0:T(8,128)(2,1)S(1)} %collective-permute-done), kind=kOutput, calls=%fused_computation.19 | convolution fusion | flops 1480196096 | bytes 12255232 | tf_op jit(solution)/shard_map/dot_general | solution.py:146
  (13 shorter events, 0.1 us)
Async XLA Ops:
  6.5 85.4 %copy-start = (bf16[896,768]{1,0:T(8,128)(2,1)S(1)}, bf16[896,768]{1,0:T(8,128)(2,1)}, u32[]{:S(2)}) copy-start(bf16[896,768]{1,0:T(8,128)(2,1)} %param.16) | copy-start | bytes 4128772
  6.5 2.2 copy-start.1
  6.5 3.4 %copy-start.5 = (s32[32]{0:T(128)S(1)}, s32[32]{0:T(128)}, u32[]{:S(2)}) copy-start(s32[32]{0:T(128)} %param.13) | copy-start | bytes 388
  6.5 79.7 %all-gather.4.cloned.1.call-start = ((), (), s32[]{:S(2)}) async-start(), calls=%async_computation.2 | async-start | bytes 7225344 | tf_op jit(solution)/shard_map/all_gather | solution.py:107
  7.3 139.1 %all-gather.8.cloned.1.call-start = ((), (), s32[]{:S(2)}) async-start(), calls=%async_computation.4 | async-start | bytes 4456448 | tf_op jit(solution)/shard_map/all_gather | solution.py:148
  8.0 211.8 %all-gather.6.cloned.1.call-start = ((), (), s32[]{:S(2)}) async-start(), calls=%async_computation.3 | async-start | bytes 7798784 | tf_op jit(solution)/shard_map/all_gather | solution.py:144
  15.8 7.8 %copy-start.4 = (bf16[896]{0:T(1024)(128)(2,1)S(1)}, bf16[896]{0:T(1024)(128)(2,1)}, u32[]{:S(2)}) copy-start(bf16[896]{0:T(1024)(128)(2,1)} %param.15) | copy-start | bytes 5380
  15.8 34.6 %all-to-all-start = ((bf16[16,16,3584]{2,1,0:T(8,128)(2,1)}), bf16[16,16,3584]{2,1,0:T(8,128)(2,1)}, u32[]{:S(2)}, u32[]{:S(2)}) async-start(bf16[16,16,3584]{2,1,0:T(8,128)(2,1)} %reshape.69), calls=%async_computation | async-start | bytes 3670016 | tf_op jit(solution)/shard_map/all_to_all | solution.py:103
  30.7 1.9 copy-start.6
  91.9 1.0 copy-start.3
  97.3 0.9 copy-start.2
  105.0 114.8 %copy-start.7 = (bf16[128,1024]{1,0:T(8,128)(2,1)S(1)}, bf16[128,1024]{1,0:T(8,128)(2,1)}, u32[]{:S(2)}) copy-start(bf16[128,1024]{1,0:T(8,128)(2,1)} %param.21) | copy-start | bytes 786436
  106.1 15.0 %all-to-all-start.1 = ((bf16[16,16,768]{2,1,0:T(8,128)(2,1)}), bf16[16,16,768]{2,1,0:T(8,128)(2,1)S(1)}, u32[]{:S(2)}, u32[]{:S(2)}) async-start(bf16[16,16,768]{2,1,0:T(8,128)(2,1)} %convert_element_type.65), calls=%async_computation.1 | async-start | bytes 786432 | tf_op jit(solution)/shard_map/all_to_all | solution.py:131
  122.0 24.4 %collective-permute-start = (bf16[128,768]{1,0:T(8,128)(2,1)S(1)}, bf16[128,768]{1,0:T(8,128)(2,1)S(1)}, u32[]{:S(2)}, u32[]{:S(2)}) collective-permute-start(bf16[128,768]{1,0:T(8,128)(2,1)S(1)} %reshape.72), channel_id=1, source_target_pairs={{0,128},{128,0},{1,129},{129,1},{2,130},{130,2},{3,131},{131,3},{4... | collective-permute-start | bytes 589832 | tf_op jit(solution)/shard_map/ppermute | solution.py:11
Sparse Core Ops, SparseCore 0:
  9.2 77.0 all-gather.3
  88.6 57.7 all-gather.7
  148.8 70.8 all-gather.5
where the time goes:
time: 235 us; the launch traced here: 234 us
  waiting for transfers between devices  155 us (66%)
  matrix products  22.2 us (9%)
  starting transfers between devices  21 us (9%)
  local copies, waits for them, and re-layouts  20.4 us (9%)
  between operations  13.4 us (6%)
    all_gather x1, waiting for transfers between devices, shards(): lax.all_gather(flow_expand_weight, 'mp', axis=0, tiled=True)  73.4 us
    all_gather x1, waiting for transfers between devices, shards(): lax.all_gather(thinker_to_talker_weight, 'dp', axis=0, tiled=True)  35.8 us
    all_to_all x1, waiting for transfers between devices, shards(): lax.all_to_all(outgoing, 'mp', split_axis=0, concat_axis=0, tiled=True)  17.8 us
    all_gather x1, waiting for transfers between devices, shards(): lax.all_gather(flow_reduce_weight, 'mp', axis=0, tiled=True)  17.8 us
    all_to_all x1, waiting for transfers between devices, shards(): lax.all_to_all(attended.reshape(mp_count, capacity * DECODE_STEPS, out_wi...  8.44 us
    dot_general x1, matrix products, shards(): jnp.dot(feedforward_hidden, lax.all_gather(flow_reduce_weight, 'mp', axis...  8.13 us
    all_to_all x1, starting transfers between devices, shards(): lax.all_to_all(outgoing, 'mp', split_axis=0, concat_axis=0, tiled=True)  7.76 us
    ppermute x1, starting transfers between devices, partner(): lax.ppermute(x, axis, [(i, i ^ 1 << apart) for i in range(lax.axis_size(a...  6.66 us
  transfers between devices with their start and end apart: 6, of which 5 were waited for; matrix products, arithmetic and copies ran while one was open for 15% of the time, Pallas kernels for 0%

commit v1 on v0

v1 whole, which is shorter than its diff:
```python
import jax
import jax.numpy as jnp
from jax import lax
from jax.experimental import pallas as pl
from jax.experimental.pallas import tpu as pltpu
from jax.sharding import PartitionSpec as P

MESH = pl.DeviceIdType.MESH
BF = jnp.bfloat16
F32 = jnp.float32
NEG = -1e30
HID = 2816
EXP = 1792


def dot(a, b):
    return jnp.dot(a, b, preferred_element_type=F32)


def dot_t(a, b):
    return lax.dot_general(a, b, (((1,), (1,)), ((), ())), preferred_element_type=F32)


def kernel(
    hid_ref, own_ref, w_ref, gain_ref, wq_ref, wk_ref, wv_ref, kv_ref, len_ref, noisy_ref, fe_ref, fr_ref,
    out_ref,
    hid, wbuf, wqkv, kbuf, vbuf, noisy, er, bias, perm, perm_t, pacc, packed, inb, qkv, outb, retb, mine, part, hpre, hact,
    lsem, t_send, t_recv, ts_send, f_send1, f_send2, f_fwd1, f_fwd2, f_recv, fs_send, fs_recv,
    a_send, a_recv, r_send, r_recv, x_send, x_recv,
):
    s = lax.axis_index("segment")
    m = lax.axis_index("mp")
    d = lax.axis_index("dp")
    zl, c = d // 2, d % 2
    z = s * 4 + zl
    y, x = m // 4, m % 4
    sib = (s, m, zl * 2 + (1 - c))

    def zdev(dz):
        zz = (z + dz + 8) % 8
        return (zz // 4, m, (zz % 4) * 2 + c)

    def xydev(dx, dy):
        return (s, ((y + dy + 4) % 4) * 4 + (x + dx + 4) % 4, d)

    def rcopy(src, dst, ss, rs, dev):
        return pltpu.make_async_remote_copy(
            src_ref=src, dst_ref=dst, send_sem=ss, recv_sem=rs, device_id=dev, device_id_type=MESH
        )

    local = []

    def load(src, dst):
        cp = pltpu.make_async_copy(src, dst, lsem.at[len(local)])
        cp.start()
        local.append(cp)
        return cp

    own_e = []
    for cc in range(2):
        for a in range(2):
            rows = pl.ds(cc * 64 + a * 32, 32)
            own_e.append(load(fe_ref.at[rows], er.at[m, cc, a, :, pl.ds(0, EXP)]))
            own_e.append(load(fr_ref.at[rows], er.at[m, cc, a, :, pl.ds(EXP, 1024)]))
    own_w = [load(w_ref.at[pl.ds(h * 224, 224)], wbuf.at[zl, c, h]) for h in range(2)]
    own_h = [load(hid_ref.at[:, pl.ds(i * 896, 896)], hid.at[i]) for i in range(4)]
    own_q = [
        load(wq_ref, wqkv.at[:, pl.ds(0, 768)]),
        load(wk_ref, wqkv.at[:, pl.ds(768, 256)]),
        load(wv_ref, wqkv.at[:, pl.ds(1024, 256)]),
    ]
    own_n = load(noisy_ref, noisy)
    own_kv = []
    for i in range(4):
        own_kv.append(load(kv_ref.at[:, i, 0], kbuf.at[:, pl.ds(i * 48, 48)]))
        own_kv.append(load(kv_ref.at[:, i, 1], vbuf.at[:, pl.ds(i * 48, 48)]))

    barrier = pltpu.get_barrier_semaphore()

    def greet(k, _):
        pl.semaphore_signal(barrier, inc=1, device_id=(s, (m + k) % 16, d), device_id_type=MESH)
        return 0

    for dev in (zdev(1), zdev(-1), sib, zdev(4)):
        pl.semaphore_signal(barrier, inc=1, device_id=dev, device_id_type=MESH)
    lax.fori_loop(1, 16, greet, 0)

    r0 = lax.broadcasted_iota(jnp.int32, (16, 208), 0)
    j0 = lax.broadcasted_iota(jnp.int32, (16, 208), 1)
    u0 = j0 - 192
    fresh_ok = (j0 >= 192) & (u0 // 4 == r0 // 4) & (u0 % 4 <= r0 % 4)
    slot0 = j0 // 48
    pos0 = j0 % 48
    same = (j0 < 192) & (slot0 == r0 // 4)

    def make_bias(g, _):
        ln = jnp.zeros((16, 208), jnp.int32)
        for i in range(4):
            ln = jnp.where(slot0 == i, len_ref[g * 4 + i], ln)
        ok = fresh_ok | (same & (pos0 < ln))
        bias[g] = jnp.where(ok, 0.0, NEG)
        return 0

    lax.fori_loop(0, 16, make_bias, 0)

    ri = lax.broadcasted_iota(jnp.int32, (128, 128), 0)
    ci = lax.broadcasted_iota(jnp.int32, (128, 128), 1)

    def owners(k, carry):
        a, b = carry
        o = own_ref[k]
        return jnp.where(ri // 4 == k, o, a), jnp.where(ci // 4 == k, o, b)

    zero = jnp.zeros((128, 128), jnp.int32)
    own_rows, own_cols = lax.fori_loop(0, 32, owners, (zero, zero))
    eq = own_rows == own_cols
    rank_row = jnp.sum(jnp.where(eq & (ri // 4 < ci // 4) & (ri % 4 == 0), 1.0, 0.0), axis=0, keepdims=True)
    rank_col = jnp.sum(jnp.where(eq & (ci // 4 < ri // 4) & (ci % 4 == 0), 1.0, 0.0), axis=1, keepdims=True)
    tgt_row = own_cols[0:1, :] * 16 + rank_row.astype(jnp.int32) * 4 + ci[0:1, :] % 4
    tgt_col = own_rows[:, 0:1] * 16 + rank_col.astype(jnp.int32) * 4 + ri[:, 0:1] % 4
    perm[...] = jnp.where(lax.broadcasted_iota(jnp.int32, (256, 128), 0) == tgt_row, 1.0, 0.0).astype(BF)
    perm_t[...] = jnp.where(lax.broadcasted_iota(jnp.int32, (128, 256), 1) == tgt_col, 1.0, 0.0).astype(BF)

    for cp in own_e:
        cp.wait()
    pl.semaphore_wait(barrier, 19)

    sends = []

    def go(cp):
        cp.start()
        sends.append(cp)

    def wcopy(zi, h, ss, dev, src=None):
        dst = wbuf.at[zi, c, h]
        return rcopy(dst if src is None else src, dst, ss, t_recv.at[zi, c, h], dev)

    for k in range(2):
        go(wcopy(zl, k, t_send.at[k], zdev(1), w_ref.at[pl.ds(k * 224, 224)]))
        go(wcopy(zl, 1 - k, t_send.at[2 + k], zdev(-1), w_ref.at[pl.ds((1 - k) * 224, 224)]))
    for k in range(2):
        go(wcopy(zl, k, ts_send.at[zl, k], sib, w_ref.at[pl.ds(k * 224, 224)]))

    def pid(a, i, j):
        return j * 4 + i if a == 0 else i * 4 + j

    def nb1(a, k):
        return xydev(k, 0) if a == 0 else xydev(0, k)

    def nb2(a, k):
        return xydev(0, k) if a == 0 else xydev(k, 0)

    def at(a):
        return (x, y) if a == 0 else (y, x)

    def full(p, a, ss, rs, dev):
        return rcopy(er.at[p, c, a], er.at[p, c, a], ss, rs, dev)

    def piece(p, a, k, ss, dev):
        ref = er.at[p, c, a, pl.ds(k * 16, 16)]
        return rcopy(ref, ref, ss, f_recv.at[p, a, k], dev)

    def got(p, a):
        full(p, a, f_send1.at[0, 0], f_recv.at[p, a, 0], sib).wait_recv()

    def got_piece(p, a, k):
        piece(p, a, k, f_send1.at[0, 0], sib).wait_recv()

    def share(p, a):
        cp = full(p, a, fs_send.at[p, a], fs_recv.at[p, a], sib)
        cp.start()

    def spread(a, i, j):
        p = pid(a, i, j)
        for k in range(2):
            full(p, a, f_send2.at[a, i, k], f_recv.at[p, a, 0], nb2(a, 1 - 2 * k)).start()

    for a in range(2):
        i, j = at(a)
        p = pid(a, i, j)
        for k in range(2):
            go(full(p, a, f_send1.at[a, k], f_recv.at[p, a, 0], nb1(a, 1 - 2 * k)))
    for a in range(2):
        spread(a, *at(a))
    for a in range(2):
        i, j = at(a)
        for k in range(2):
            i1 = (i + (3 if k == 0 else 1)) % 4
            p = pid(a, i1, j)
            got(p, a)
            go(piece(p, a, k, f_fwd1.at[a, k], nb1(a, 1 - 2 * k)))
            spread(a, i1, j)
            share(p, a)
    for a in range(2):
        i, j = at(a)
        i2 = (i + 2) % 4
        p = pid(a, i2, j)
        got_piece(p, a, 0)
        got_piece(p, a, 1)
        spread(a, i2, j)
        share(p, a)

    for cp in own_h + own_w:
        cp.wait()
    zm, zp, z2 = (zl + 3) % 4, (zl + 1) % 4, (zl + 2) % 4

    def wgot(zi, cc, h):
        dst = wbuf.at[zi, cc, h]
        rcopy(dst, dst, t_send.at[0], t_recv.at[zi, cc, h], sib).wait_recv()

    def wshare(zi, h):
        dst = wbuf.at[zi, c, h]
        rcopy(dst, dst, ts_send.at[zi, h], t_recv.at[zi, c, h], sib).start()

    def second(t, _):
        for a in range(2):
            i, j = at(a)
            it = (i + t) % 4
            for k in range(2):
                p = pid(a, it, (j + (3 if k == 0 else 1)) % 4)
                got(p, a)
                piece(p, a, k, f_fwd2.at[a, it, k], nb2(a, 1 - 2 * k)).start()
                share(p, a)
        return 0

    lax.fori_loop(0, 2, second, 0)
    for h in range(2):
        wgot(zl, 1 - c, h)
    pacc[...] = dot(hid[zl], wbuf[zl].reshape(896, 896))
    wgot(zm, c, 0)
    go(wcopy(zm, 0, t_send.at[4], zdev(1)))
    wgot(zp, c, 1)
    go(wcopy(zp, 1, t_send.at[5], zdev(-1)))
    wshare(zm, 0)
    wshare(zp, 1)
    lax.fori_loop(2, 4, second, 0)
    wgot(zm, c, 1)
    wshare(zm, 1)
    wgot(zp, c, 0)
    wshare(zp, 0)
    for zi in (zm, zp):
        for h in range(2):
            wgot(zi, 1 - c, h)
        pacc[...] += dot(hid[zi], wbuf[zi].reshape(896, 896))
    for h in range(2):
        wgot(z2, c, h)
        wshare(z2, h)
    for h in range(2):
        wgot(z2, 1 - c, h)
    projected = (pacc[...] + dot(hid[z2], wbuf[z2].reshape(896, 896))).astype(BF).astype(F32)
    scale = lax.rsqrt(jnp.mean(projected * projected, axis=-1, keepdims=True) + 1e-06)
    normed = (projected * scale * gain_ref[...].astype(F32)).astype(BF)
    packed[...] = dot(perm[...], normed).astype(BF).reshape(16, 16, 896)

    def post(k, _):
        o = (m + k) % 16
        rcopy(packed.at[o], inb.at[m], a_send.at[o], a_recv.at[m], (s, o, d)).start()
        return 0

    lax.fori_loop(1, 16, post, 0)
    inb[m] = packed[m]

    def third(t, _):
        for a in range(2):
            i, j = at(a)
            p = pid(a, (i + t) % 4, (j + 2) % 4)
            got_piece(p, a, 0)
            got_piece(p, a, 1)
            share(p, a)
        return 0

    lax.fori_loop(0, 4, third, 0)
    for cp in own_q + own_kv + [own_n]:
        cp.wait()

    def arrive(k, _):
        o = (m + k) % 16
        rcopy(packed.at[o], inb.at[o], a_send.at[o], a_recv.at[o], (s, o, d)).wait()
        return 0

    lax.fori_loop(1, 16, arrive, 0)
    qkv[...] = dot(inb[...].reshape(256, 896), wqkv[...]).astype(BF).reshape(16, 16, 1280)
    kbuf[:, 192:208, :] = qkv[:, :, 768:1024]
    vbuf[:, 192:208, :] = qkv[:, :, 1024:1280]

    factor = 128 ** (-0.5)

    def attend(q4, _):
        for gg in range(4):
            g = q4 * 4 + gg
            for h in range(2):
                q = jnp.concatenate(
                    [qkv[g, :, (h * 3 + e) * 128 : (h * 3 + e + 1) * 128] for e in range(3)], axis=0
                )
                sc = dot_t(q, kbuf[g, :, h * 128 : (h + 1) * 128]) * factor
                sc = sc.reshape(3, 16, 208) + bias[g][None]
                pk = jnp.max(sc, axis=-1, keepdims=True)
                pr = jnp.exp(sc - pk)
                wt = (pr / jnp.sum(pr, axis=-1, keepdims=True)).astype(BF)
                o = dot(wt.reshape(48, 208), vbuf[g, :, h * 128 : (h + 1) * 128]).astype(BF)
                for e in range(3):
                    outb[g, :, (h * 3 + e) * 128 : (h * 3 + e + 1) * 128] = o[e * 16 : (e + 1) * 16]
        for gg in range(4):
            g = q4 * 4 + gg

            @pl.when(g != m)
            def _():
                rcopy(outb.at[g], retb.at[m], r_send.at[g], r_recv.at[m], (s, g, d)).start()

        return 0

    lax.fori_loop(0, 4, attend, 0)
    retb[m] = outb[m]

    def back(k, _):
        o = (m + k) % 16
        rcopy(outb.at[o], retb.at[o], r_send.at[o], r_recv.at[o], (s, o, d)).wait()
        return 0

    lax.fori_loop(1, 16, back, 0)
    mine[...] = dot(perm_t[...], retb[...].reshape(256, 768)).astype(BF)
    swap = rcopy(mine, part, x_send.at[0], x_recv.at[0], zdev(4))
    swap.start()

    def shared(t, _):
        p = (m + t) % 16
        for a in range(2):
            dst = er.at[p, 1 - c, a]
            rcopy(dst, dst, fs_send.at[p, a], fs_recv.at[p, a], sib).wait_recv()
            full(p, a, fs_send.at[p, a], fs_recv.at[p, a], sib).wait_send()
        return 0

    lax.fori_loop(1, 16, shared, 0)

    def early(t, _):
        e = er[pl.ds(t * 2, 2), :, :, :, 0:1024].reshape(256, 1024)
        hpre[t] = dot_t(noisy[...], e)
        return 0

    lax.fori_loop(0, 8, early, 0)
    swap.wait()

    def late(t, _):
        e = er[pl.ds(t * 2, 2), :, :, :, 1024:EXP].reshape(256, 768)
        hact[t] = jax.nn.gelu(hpre[t] + dot_t(part[...], e)).astype(BF)
        return 0

    lax.fori_loop(0, 8, late, 0)
    h = jnp.concatenate([hact[t] for t in range(8)], axis=1)
    for n in range(4):
        cols = slice(n * 256, (n + 1) * 256)
        r = er[:, :, :, :, EXP + n * 256 : EXP + (n + 1) * 256].reshape(2048, 256)
        out_ref[:, cols] = (noisy[:, cols].astype(F32) + 0.5 * dot(h, r)).astype(BF)

    for cp in sends:
        cp.wait_send()
    for zi in (zm, zp, z2):
        for hh in range(2):
            dst = wbuf.at[zi, c, hh]
            rcopy(dst, dst, ts_send.at[zi, hh], t_recv.at[zi, c, hh], sib).wait_send()

    def sent(i, _):
        for a in range(2):
            p = pid(a, i, at(a)[1])
            for k in range(2):
                full(p, a, f_send2.at[a, i, k], f_recv.at[p, a, 0], sib).wait_send()
                piece(p, a, k, f_fwd2.at[a, i, k], sib).wait_send()
        return 0

    lax.fori_loop(0, 4, sent, 0)


def shards(hidden, owner, w, gain, wq, wk, wv, cache, fill, noisy, fe, fr):
    any_ = pl.BlockSpec(memory_space=pl.ANY)
    smem = pl.BlockSpec(memory_space=pltpu.SMEM)
    vmem = pl.BlockSpec(memory_space=pltpu.VMEM)
    dma = pltpu.SemaphoreType.DMA
    return pl.pallas_call(
        kernel,
        out_shape=jax.ShapeDtypeStruct((128, 1024), BF),
        in_specs=[any_, smem, any_, vmem, any_, any_, any_, any_, smem, any_, any_, any_],
        out_specs=vmem,
        scratch_shapes=[
            pltpu.VMEM((4, 128, 896), BF),
            pltpu.VMEM((4, 2, 2, 224, 896), BF),
            pltpu.VMEM((896, 1280), BF),
            pltpu.VMEM((16, 208, 256), BF),
            pltpu.VMEM((16, 208, 256), BF),
            pltpu.VMEM((128, 1024), BF),
            pltpu.VMEM((16, 2, 2, 32, HID), BF),
            pltpu.VMEM((16, 16, 208), F32),
            pltpu.VMEM((256, 128), BF),
            pltpu.VMEM((128, 256), BF),
            pltpu.VMEM((128, 896), F32),
            pltpu.VMEM((16, 16, 896), BF),
            pltpu.VMEM((16, 16, 896), BF),
            pltpu.VMEM((16, 16, 1280), BF),
            pltpu.VMEM((16, 16, 768), BF),
            pltpu.VMEM((16, 16, 768), BF),
            pltpu.VMEM((128, 768), BF),
            pltpu.VMEM((128, 768), BF),
            pltpu.VMEM((8, 128, 256), F32),
            pltpu.VMEM((8, 128, 256), BF),
            dma((32,)),
            dma((6,)),
            dma((4, 2, 2)),
            dma((4, 2)),
            dma((2, 2)),
            dma((2, 4, 2)),
            dma((2, 2)),
            dma((2, 4, 2)),
            dma((16, 2, 2)),
            dma((16, 2)),
            dma((16, 2)),
            dma((16,)),
            dma((16,)),
            dma((16,)),
            dma((16,)),
            dma((1,)),
            dma((1,)),
        ],
        compiler_params=pltpu.CompilerParams(
            collective_id=0, has_side_effects=True, vmem_limit_bytes=50 * 2**20
        ),
        name="talker_flow",
    )(
        hidden, owner, w, gain.reshape(1, 896), wq, wk, wv, cache.reshape(16, 4, 2, 48, 256), fill, noisy, fe, fr,
    )


def solution(mesh):
    placed = (
        P(("segment", "mp", "dp"), None),
        P(("segment", "mp", "dp")),
        P("dp", None),
        P(),
        P(),
        P(),
        P(),
        P(("segment", "mp", "dp"), None, None, None),
        P(("segment", "mp", "dp")),
        P(("segment", "mp", "dp"), None),
        P("mp", None),
        P("mp", None),
    )
    return jax.shard_map(
        shards,
        mesh=mesh,
        in_specs=placed,
        out_specs=P(("segment", "mp", "dp"), None),
        check_vma=False,
    )
```

time: 235 us -> 95.3 us (0.41)
  the two profiles are of different devices: /device:TPU:1 before, /device:TPU:30 now
where the time goes in v1:
time: 95.3 us; the launch traced here: 94.9 us
  Pallas kernels  84.9 us (89%)
  local copies, waits for them, and re-layouts  9.97 us (10%)
    pallas_call x1, Pallas kernels, shards(): pl.pallas_call(kernel, out_shape=jax.ShapeDtypeStruct((128, 1024), BF), i...  84.9 us
    unnamed x19, local copies, waits for them, and re-layouts  9.28 us

profile of v1, /device:TPU:30, one launch (start us, length us, event | category | flops | bytes accessed | tf_op | source)
XLA Modules:
  0.0 94.9 jit_solution(15771823041995658807)
XLA Ops:
  0.0 0.7 reshape.6.gain_ref
  0.7 0.0 copy-start
  0.7 1.2 %copy-done = bf16[128,3584]{1,0:T(8,128)(2,1)S(1)} copy-done((bf16[128,3584]{1,0:T(8,128)(2,1)S(1)}, bf16[128,3584]{1,0:T(8,128)(2,1)}, u32[]{:S(2)}) %copy-start) | copy-done | bytes 917528
  1.9 0.0 copy-start.1
  1.9 1.1 %copy-done.1 = bf16[448,896]{1,0:T(8,128)(2,1)S(1)} copy-done((bf16[448,896]{1,0:T(8,128)(2,1)S(1)}, bf16[448,896]{1,0:T(8,128)(2,1)}, u32[]{:S(2)}) %copy-start.1) | copy-done | bytes 802840
  3.0 0.0 copy-start.2
  3.0 1.0 %copy-done.2 = bf16[896,256]{1,0:T(8,128)(2,1)S(1)} copy-done((bf16[896,256]{1,0:T(8,128)(2,1)S(1)}, bf16[896,256]{1,0:T(8,128)(2,1)}, u32[]{:S(2)}) %copy-start.2) | copy-done | bytes 458776
  4.0 0.0 copy-start.3
  4.0 1.0 %copy-done.3 = bf16[896,256]{1,0:T(8,128)(2,1)S(1)} copy-done((bf16[896,256]{1,0:T(8,128)(2,1)S(1)}, bf16[896,256]{1,0:T(8,128)(2,1)}, u32[]{:S(2)}) %copy-start.3) | copy-done | bytes 458776
  5.0 0.0 copy-start.4
  5.0 1.0 %copy-done.4 = bf16[128,1792]{1,0:T(8,128)(2,1)S(1)} copy-done((bf16[128,1792]{1,0:T(8,128)(2,1)S(1)}, bf16[128,1792]{1,0:T(8,128)(2,1)}, u32[]{:S(2)}) %copy-start.4) | copy-done | bytes 458776
  6.1 0.0 copy-start.5
  6.1 0.9 copy-done.5
  7.0 0.0 copy-start.6
  7.0 0.9 copy-done.6
  8.0 0.0 copy-start.7
  8.0 0.7 copy-done.7
  8.6 0.0 copy-start.8
  8.6 0.7 copy-done.8
  9.3 84.9 %talker_flow.1 = bf16[128,1024]{1,0:T(8,128)(2,1)S(1)} custom-call(bf16[128,3584]{1,0:T(8,128)(2,1)S(1)} %copy-done, s32[32]{0:T(128)S(1)} %copy-done.7, bf16[448,896]{1,0:T(8,128)(2,1)S(1)} %copy-done.1, bf16[1,896]{1,0:T(2,128)(2,1)S(1)} %reshape.6.gain_ref, bf16[896,768]{1,0:T(8,128)(2,1)} %wq_ref.1, bf16[896,256]{1,0:T(8,128)(2,1)S(1)} %copy-done.2, ...), custom_call_target="tpu_custom_call" | custom-call | tf_op jit(solution)/shard_map/talker_flow/pallas_call | solution.py:378
  94.2 0.7 copy.14
Async XLA Ops:
  0.7 1.2 %copy-start = (bf16[128,3584]{1,0:T(8,128)(2,1)S(1)}, bf16[128,3584]{1,0:T(8,128)(2,1)}, u32[]{:S(2)}) copy-start(bf16[128,3584]{1,0:T(8,128)(2,1)} %hid_ref.1) | copy-start | bytes 2752516
  1.9 1.1 %copy-start.1 = (bf16[448,896]{1,0:T(8,128)(2,1)S(1)}, bf16[448,896]{1,0:T(8,128)(2,1)}, u32[]{:S(2)}) copy-start(bf16[448,896]{1,0:T(8,128)(2,1)} %w_ref.1) | copy-start | bytes 2408452
  3.0 1.0 %copy-start.2 = (bf16[896,256]{1,0:T(8,128)(2,1)S(1)}, bf16[896,256]{1,0:T(8,128)(2,1)}, u32[]{:S(2)}) copy-start(bf16[896,256]{1,0:T(8,128)(2,1)} %wk_ref.1) | copy-start | bytes 1376260
  4.0 1.0 %copy-start.3 = (bf16[896,256]{1,0:T(8,128)(2,1)S(1)}, bf16[896,256]{1,0:T(8,128)(2,1)}, u32[]{:S(2)}) copy-start(bf16[896,256]{1,0:T(8,128)(2,1)} %wv_ref.1) | copy-start | bytes 1376260
  5.0 1.0 %copy-start.4 = (bf16[128,1792]{1,0:T(8,128)(2,1)S(1)}, bf16[128,1792]{1,0:T(8,128)(2,1)}, u32[]{:S(2)}) copy-start(bf16[128,1792]{1,0:T(8,128)(2,1)} %fe_ref.1) | copy-start | bytes 1376260
  6.1 0.9 %copy-start.5 = (bf16[128,1024]{1,0:T(8,128)(2,1)S(1)}, bf16[128,1024]{1,0:T(8,128)(2,1)}, u32[]{:S(2)}) copy-start(bf16[128,1024]{1,0:T(8,128)(2,1)} %noisy_ref.1) | copy-start | bytes 786436
  7.0 0.9 %copy-start.6 = (bf16[128,1024]{1,0:T(8,128)(2,1)S(1)}, bf16[128,1024]{1,0:T(8,128)(2,1)}, u32[]{:S(2)}) copy-start(bf16[128,1024]{1,0:T(8,128)(2,1)} %fr_ref.1) | copy-start | bytes 786436
  8.0 0.7 copy-start.7
  8.6 0.7 copy-start.8

commit v2 on v1

--- a/solution.py
+++ b/solution.py
@@ -22,9 +22,9 @@
 
 
 def kernel(
-    hid_ref, own_ref, w_ref, gain_ref, wq_ref, wk_ref, wv_ref, kv_ref, len_ref, noisy_ref, fe_ref, fr_ref,
+    hid_ref, own_hbm, w_ref, gain_ref, wq_ref, wk_ref, wv_ref, kv_ref, len_hbm, noisy_ref, fe_ref, fr_ref,
     out_ref,
-    hid, wbuf, wqkv, kbuf, vbuf, noisy, er, bias, perm, perm_t, pacc, packed, inb, qkv, outb, retb, mine, part, hpre, hact,
+    own_ref, len_ref, hid, wbuf, wqkv, kbuf, vbuf, noisy, er, bias, perm, perm_t, pacc, packed, inb, qkv, outb, retb, mine, part, hpre, hact,
     lsem, t_send, t_recv, ts_send, f_send1, f_send2, f_fwd1, f_fwd2, f_recv, fs_send, fs_recv,
     a_send, a_recv, r_send, r_recv, x_send, x_recv,
 ):
@@ -48,6 +48,16 @@
             src_ref=src, dst_ref=dst, send_sem=ss, recv_sem=rs, device_id=dev, device_id_type=MESH
         )
 
+    barrier = pltpu.get_barrier_semaphore()
+
+    def greet(k, _):
+        pl.semaphore_signal(barrier, inc=1, device_id=(s, (m + k) % 16, d), device_id_type=MESH)
+        return 0
+
+    for dev in (zdev(1), zdev(-1), sib, zdev(4)):
+        pl.semaphore_signal(barrier, inc=1, device_id=dev, device_id_type=MESH)
+    lax.fori_loop(1, 16, greet, 0)
+
     local = []
 
     def load(src, dst):
@@ -56,6 +66,7 @@
         local.append(cp)
         return cp
 
+    own_s = [load(own_hbm, own_ref), load(len_hbm, len_ref)]
     own_e = []
     for cc in range(2):
         for a in range(2):
@@ -75,16 +86,8 @@
         own_kv.append(load(kv_ref.at[:, i, 0], kbuf.at[:, pl.ds(i * 48, 48)]))
         own_kv.append(load(kv_ref.at[:, i, 1], vbuf.at[:, pl.ds(i * 48, 48)]))
 
-    barrier = pltpu.get_barrier_semaphore()
-
-    def greet(k, _):
-        pl.semaphore_signal(barrier, inc=1, device_id=(s, (m + k) % 16, d), device_id_type=MESH)
-        return 0
-
-    for dev in (zdev(1), zdev(-1), sib, zdev(4)):
-        pl.semaphore_signal(barrier, inc=1, device_id=dev, device_id_type=MESH)
-    lax.fori_loop(1, 16, greet, 0)
-
+    for cp in own_s:
+        cp.wait()
     r0 = lax.broadcasted_iota(jnp.int32, (16, 208), 0)
     j0 = lax.broadcasted_iota(jnp.int32, (16, 208), 1)
     u0 = j0 - 192
@@ -249,7 +252,7 @@
         wgot(z2, 1 - c, h)
     projected = (pacc[...] + dot(hid[z2], wbuf[z2].reshape(896, 896))).astype(BF).astype(F32)
     scale = lax.rsqrt(jnp.mean(projected * projected, axis=-1, keepdims=True) + 1e-06)
-    normed = (projected * scale * gain_ref[...].astype(F32)).astype(BF)
+    normed = (projected * scale * gain_ref[...].astype(F32).reshape(1, 896)).astype(BF)
     packed[...] = dot(perm[...], normed).astype(BF).reshape(16, 16, 896)
 
     def post(k, _):
@@ -285,42 +288,47 @@
 
     factor = 128 ** (-0.5)
 
-    def attend(q4, _):
-        for gg in range(4):
-            g = q4 * 4 + gg
-            for h in range(2):
-                q = jnp.concatenate(
-                    [qkv[g, :, (h * 3 + e) * 128 : (h * 3 + e + 1) * 128] for e in range(3)], axis=0
-                )
-                sc = dot_t(q, kbuf[g, :, h * 128 : (h + 1) * 128]) * factor
-                sc = sc.reshape(3, 16, 208) + bias[g][None]
-                pk = jnp.max(sc, axis=-1, keepdims=True)
-                pr = jnp.exp(sc - pk)
-                wt = (pr / jnp.sum(pr, axis=-1, keepdims=True)).astype(BF)
-                o = dot(wt.reshape(48, 208), vbuf[g, :, h * 128 : (h + 1) * 128]).astype(BF)
+    def give(h, g):
+        return rcopy(outb.at[h, g], retb.at[h, m], r_send.at[h, g], r_recv.at[h, m], (s, g, d))
+
+    for h in range(2):
+        kcols = slice(h * 128, (h + 1) * 128)
+        for q4 in range(4):
+            group = range(q4 * 4, q4 * 4 + 4)
+            sc = []
+            for g in group:
+                q = [qkv[g, :, (h * 3 + e) * 128 : (h * 3 + e + 1) * 128] for e in range(3)]
+                sc.append(dot_t(jnp.concatenate(q, axis=0), kbuf[g, :, kcols]).reshape(3, 16, 208))
+            sc = jnp.stack(sc) * factor + bias[q4 * 4 : q4 * 4 + 4][:, None]
+            pr = jnp.exp(sc - jnp.max(sc, axis=-1, keepdims=True))
+            inv = (1.0 / jnp.sum(pr, axis=-1, keepdims=True)).reshape(4, 48, 1)
+            pr = pr.astype(BF).reshape(4, 48, 208)
+            for gg, g in enumerate(group):
+                o = (dot(pr[gg], vbuf[g, :, kcols]) * inv[gg]).astype(BF)
                 for e in range(3):
-                    outb[g, :, (h * 3 + e) * 128 : (h * 3 + e + 1) * 128] = o[e * 16 : (e + 1) * 16]
-        for gg in range(4):
-            g = q4 * 4 + gg
-
-            @pl.when(g != m)
-            def _():
-                rcopy(outb.at[g], retb.at[m], r_send.at[g], r_recv.at[m], (s, g, d)).start()
-
-        return 0
-
-    lax.fori_loop(0, 4, attend, 0)
-    retb[m] = outb[m]
-
-    def back(k, _):
-        o = (m + k) % 16
-        rcopy(outb.at[o], retb.at[o], r_send.at[o], r_recv.at[o], (s, o, d)).wait()
-        return 0
-
-    lax.fori_loop(1, 16, back, 0)
-    mine[...] = dot(perm_t[...], retb[...].reshape(256, 768)).astype(BF)
-    swap = rcopy(mine, part, x_send.at[0], x_recv.at[0], zdev(4))
-    swap.start()
+                    outb[h, g, :, e * 128 : (e + 1) * 128] = o[e * 16 : (e + 1) * 16]
+
+            def give4(g, _):
+                @pl.when(g != m)
+                def _():
+                    give(h, g).start()
+
+                return 0
+
+            lax.fori_loop(q4 * 4, q4 * 4 + 4, give4, 0)
+        retb[h, m] = outb[h, m]
+    swaps = []
+    for h in range(2):
+
+        def back(k, _):
+            o = (m + k) % 16
+            rcopy(outb.at[h, o], retb.at[h, o], r_send.at[h, o], r_recv.at[h, o], (s, o, d)).wait()
+            return 0
+
+        lax.fori_loop(1, 16, back, 0)
+        mine[h] = dot(perm_t[...], retb[h].reshape(256, 384)).astype(BF)
+        swaps.append(rcopy(mine.at[h], part.at[h], x_send.at[h], x_recv.at[h], zdev(4)))
+        swaps[h].start()
 
     def shared(t, _):
         p = (m + t) % 16
@@ -338,14 +346,22 @@
         return 0
 
     lax.fori_loop(0, 8, early, 0)
-    swap.wait()
-
-    def late(t, _):
-        e = er[pl.ds(t * 2, 2), :, :, :, 1024:EXP].reshape(256, 768)
-        hact[t] = jax.nn.gelu(hpre[t] + dot_t(part[...], e)).astype(BF)
-        return 0
-
-    lax.fori_loop(0, 8, late, 0)
+    swaps[0].wait()
+
+    def late0(t, _):
+        e = er[pl.ds(t * 2, 2), :, :, :, 1024:1408].reshape(256, 384)
+        hpre[t] += dot_t(part[0], e)
+        return 0
+
+    lax.fori_loop(0, 8, late0, 0)
+    swaps[1].wait()
+
+    def late1(t, _):
+        e = er[pl.ds(t * 2, 2), :, :, :, 1408:EXP].reshape(256, 384)
+        hact[t] = jax.nn.gelu(hpre[t] + dot_t(part[1], e)).astype(BF)
+        return 0
+
+    lax.fori_loop(0, 8, late1, 0)
     h = jnp.concatenate([hact[t] for t in range(8)], axis=1)
     for n in range(4):
         cols = slice(n * 256, (n + 1) * 256)
@@ -372,15 +388,16 @@
 
 def shards(hidden, owner, w, gain, wq, wk, wv, cache, fill, noisy, fe, fr):
     any_ = pl.BlockSpec(memory_space=pl.ANY)
-    smem = pl.BlockSpec(memory_space=pltpu.SMEM)
     vmem = pl.BlockSpec(memory_space=pltpu.VMEM)
     dma = pltpu.SemaphoreType.DMA
     return pl.pallas_call(
         kernel,
         out_shape=jax.ShapeDtypeStruct((128, 1024), BF),
-        in_specs=[any_, smem, any_, vmem, any_, any_, any_, any_, smem, any_, any_, any_],
+        in_specs=[any_, any_, any_, vmem, any_, any_, any_, any_, any_, any_, any_, any_],
         out_specs=vmem,
         scratch_shapes=[
+            pltpu.SMEM((32,), jnp.int32),
+            pltpu.SMEM((64,), jnp.int32),
             pltpu.VMEM((4, 128, 896), BF),
             pltpu.VMEM((4, 2, 2, 224, 896), BF),
             pltpu.VMEM((896, 1280), BF),
@@ -395,10 +412,10 @@
             pltpu.VMEM((16, 16, 896), BF),
             pltpu.VMEM((16, 16, 896), BF),
             pltpu.VMEM((16, 16, 1280), BF),
-            pltpu.VMEM((16, 16, 768), BF),
-            pltpu.VMEM((16, 16, 768), BF),
-            pltpu.VMEM((128, 768), BF),
-            pltpu.VMEM((128, 768), BF),
+            pltpu.VMEM((2, 16, 16, 384), BF),
+            pltpu.VMEM((2, 16, 16, 384), BF),
+            pltpu.VMEM((2, 128, 384), BF),
+            pltpu.VMEM((2, 128, 384), BF),
             pltpu.VMEM((8, 128, 256), F32),
             pltpu.VMEM((8, 128, 256), BF),
             dma((32,)),
@@ -414,17 +431,17 @@
             dma((16, 2)),
             dma((16,)),
             dma((16,)),
-            dma((16,)),
-            dma((16,)),
-            dma((1,)),
-            dma((1,)),
+            dma((2, 16)),
+            dma((2, 16)),
+            dma((2,)),
+            dma((2,)),
         ],
         compiler_params=pltpu.CompilerParams(
-            collective_id=0, has_side_effects=True, vmem_limit_bytes=50 * 2**20
+            collective_id=0, has_side_effects=True, vmem_limit_bytes=63 * 2**20
         ),
         name="talker_flow",
     )(
-        hidden, owner, w, gain.reshape(1, 896), wq, wk, wv, cache.reshape(16, 4, 2, 48, 256), fill, noisy, fe, fr,
+        hidden, owner, w, gain, wq, wk, wv, cache.reshape(16, 4, 2, 48, 256), fill, noisy, fe, fr,
     )
 
 

time: 95.3 us -> 76 us (0.80)
  the two profiles are of different devices: /device:TPU:30 before, /device:TPU:16 now
where the time goes in v2:
time: 76 us; the launch traced here: 75.9 us
  Pallas kernels  74.2 us (98%)
  local copies, waits for them, and re-layouts  1.67 us (2%)
    pallas_call x1, Pallas kernels, shards(): pl.pallas_call(kernel, out_shape=jax.ShapeDtypeStruct((128, 1024), BF), i...  74.2 us
    unnamed x1, local copies, waits for them, and re-layouts  1.67 us

profile of v2, /device:TPU:16, one launch (start us, length us, event | category | flops | bytes accessed | tf_op | source)
XLA Modules:
  0.0 75.9 jit_solution(16047164499341154946)
XLA Ops:
  0.0 74.2 %talker_flow.1 = bf16[128,1024]{1,0:T(8,128)(2,1)} custom-call(bf16[128,3584]{1,0:T(8,128)(2,1)} %hid_ref.1, s32[32]{0:T(128)} %own_hbm.1, bf16[448,896]{1,0:T(8,128)(2,1)} %w_ref.1, bf16[896]{0:T(1024)(128)(2,1)} %gain_ref.1, bf16[896,768]{1,0:T(8,128)(2,1)} %wq_ref.1, bf16[896,256]{1,0:T(8,128)(2,1)} %wk_ref.1, bf16[896,256]{1,0:T(8,128)(2,1)} %wv_ref.1, ...), custom_call_target="tpu_custom_call" | custom-call | tf_op jit(solution)/shard_map/talker_flow/pallas_call | solution.py:393
  74.2 1.7 %copy.14 = bf16[128,1024]{1,0:T(8,128)(2,1)} copy(bf16[128,1024]{1,0:T(8,128)(2,1)} %talker_flow.1) | data formatting | bytes 524288

commit v3 on v2

v3 whole, which is shorter than its diff:
```python
import jax
import jax.numpy as jnp
from jax import lax
from jax.experimental import pallas as pl
from jax.experimental.pallas import tpu as pltpu
from jax.sharding import PartitionSpec as P

MESH = pl.DeviceIdType.MESH
BF = jnp.bfloat16
F32 = jnp.float32
NEG = -1e30
EXP = 1792


def dot(a, b):
    return jnp.dot(a, b, preferred_element_type=F32)


def dot_t(a, b):
    return lax.dot_general(a, b, (((1,), (1,)), ((), ())), preferred_element_type=F32)


def kernel(
    hid_ref, own_hbm, w_ref, gain_ref, wq_ref, wk_ref, wv_ref, kv_ref, len_hbm, noisy_ref, fe_ref, fr_ref,
    out_ref,
    own_ref, len_ref, hid, hin, pout, pin, wown, wqkv, kbuf, vbuf, noisy, eb, rb, bias, perm, perm_t, pacc, packed, inb, qkv, outb, retb, mine, part, hpre, hact,
    lsem, w_send, w_recv, h_send, h_recv, p_send, p_recv, f_send1, f_send2, f_fwd1, f_fwd2, f_recv, fs_send, fs_recv,
    a_send, a_recv, r_send, r_recv, x_send, x_recv,
):
    s = lax.axis_index("segment")
    m = lax.axis_index("mp")
    d = lax.axis_index("dp")
    zl, c = d // 2, d % 2
    z = s * 4 + zl
    y, x = m // 4, m % 4
    sib = (s, m, zl * 2 + (1 - c))

    def zdev(dz):
        zz = (z + dz + 8) % 8
        return (zz // 4, m, (zz % 4) * 2 + c)

    def xydev(dx, dy):
        return (s, ((y + dy + 4) % 4) * 4 + (x + dx + 4) % 4, d)

    def rcopy(src, dst, ss, rs, dev):
        return pltpu.make_async_remote_copy(
            src_ref=src, dst_ref=dst, send_sem=ss, recv_sem=rs, device_id=dev, device_id_type=MESH
        )

    barrier = pltpu.get_barrier_semaphore()

    def greet(k, _):
        pl.semaphore_signal(barrier, inc=1, device_id=(s, (m + k) % 16, d), device_id_type=MESH)
        return 0

    for dev in (zdev(1), zdev(-1), zdev(2), zdev(-2), zdev(4), sib):
        pl.semaphore_signal(barrier, inc=1, device_id=dev, device_id_type=MESH)
    lax.fori_loop(1, 16, greet, 0)

    local = []

    def load(src, dst):
        cp = pltpu.make_async_copy(src, dst, lsem.at[len(local)])
        cp.start()
        local.append(cp)
        return cp

    own_s = [load(own_hbm, own_ref), load(len_hbm, len_ref)]
    own_e = []
    for cc in range(2):
        for a in range(2):
            rows = pl.ds(cc * 64 + a * 32, 32)
            own_e.append(load(fe_ref.at[rows], eb.at[m, cc, a]))
            own_e.append(load(fr_ref.at[rows], rb.at[m, cc, a]))
    own_w = load(w_ref, wown.at[c])
    own_h = load(hid_ref.at[:, pl.ds(pl.multiple_of(zl * 896, 128), 896)], hid)
    own_q = [
        load(wq_ref, wqkv.at[:, pl.ds(0, 768)]),
        load(wk_ref, wqkv.at[:, pl.ds(768, 256)]),
        load(wv_ref, wqkv.at[:, pl.ds(1024, 256)]),
    ]
    own_n = load(noisy_ref, noisy)
    own_kv = []
    for i in range(4):
        own_kv.append(load(kv_ref.at[:, i, 0], kbuf.at[:, pl.ds(i * 48, 48)]))
        own_kv.append(load(kv_ref.at[:, i, 1], vbuf.at[:, pl.ds(i * 48, 48)]))

    pl.semaphore_wait(barrier, 21)

    sends = []

    def go(cp):
        cp.start()
        sends.append(cp)

    two = 2 - 4 * c
    steps = (two, 1, -1)

    def hcopy(k, dz):
        cols = pl.ds(pl.multiple_of((zl + dz + 4) % 4 * 896, 128), 896)
        return rcopy(hid_ref.at[:, cols], hin.at[k], h_send.at[k], h_recv.at[k], zdev(dz))

    def pcopy(k, dz):
        return rcopy(pout.at[k], pin.at[k], p_send.at[k], p_recv.at[k], zdev(-dz))

    def own_weight(cc):
        return rcopy(w_ref, wown.at[cc], w_send.at[0], w_recv.at[0], sib)

    for k, dz in enumerate(steps):
        go(hcopy(k, dz))
    go(own_weight(c))

    def pid(a, i, j):
        return j * 4 + i if a == 0 else i * 4 + j

    def nb1(a, k):
        return xydev(k, 0) if a == 0 else xydev(0, k)

    def nb2(a, k):
        return xydev(0, k) if a == 0 else xydev(k, 0)

    def at(a):
        return (x, y) if a == 0 else (y, x)

    class Gather:
        def __init__(self, n, buf):
            self.n, self.buf = n, buf

        def full(self, p, a, ss, rs, dev):
            return rcopy(self.buf.at[p, c, a], self.buf.at[p, c, a], ss, rs, dev)

        def piece(self, p, a, k, ss, dev):
            ref = self.buf.at[p, c, a, pl.ds(k * 16, 16)]
            return rcopy(ref, ref, ss, f_recv.at[self.n, p, a, k], dev)

        def got(self, p, a):
            self.full(p, a, f_send1.at[self.n, 0, 0], f_recv.at[self.n, p, a, 0], sib).wait_recv()

        def got_pieces(self, p, a):
            for k in range(2):
                self.piece(p, a, k, f_send1.at[self.n, 0, 0], sib).wait_recv()

        def share(self, p, a):
            self.full(p, a, fs_send.at[self.n, p, a], fs_recv.at[self.n, p, a], sib).start()

        def spread(self, a, i, j):
            p = pid(a, i, j)
            for k in range(2):
                sems = f_send2.at[self.n, a, i, k], f_recv.at[self.n, p, a, 0]
                self.full(p, a, *sems, nb2(a, 1 - 2 * k)).start()

        def begin(self):
            for a in range(2):
                p = pid(a, *at(a))
                for k in range(2):
                    sems = f_send1.at[self.n, a, k], f_recv.at[self.n, p, a, 0]
                    go(self.full(p, a, *sems, nb1(a, 1 - 2 * k)))

        def begin2(self):
            for a in range(2):
                self.spread(a, *at(a))

        def first(self):
            for a in range(2):
                i, j = at(a)
                for k in range(2):
                    p = pid(a, (i + (3 if k == 0 else 1)) % 4, j)
                    self.got(p, a)
                    go(self.piece(p, a, k, f_fwd1.at[self.n, a, k], nb1(a, 1 - 2 * k)))

        def first_spread(self):
            for a in range(2):
                i, j = at(a)
                for k in (1, 3):
                    self.spread(a, (i + k) % 4, j)
                    self.share(pid(a, (i + k) % 4, j), a)

        def first_far(self):
            for a in range(2):
                i, j = at(a)
                i2 = (i + 2) % 4
                self.got_pieces(pid(a, i2, j), a)
                self.spread(a, i2, j)
                self.share(pid(a, i2, j), a)

        def second(self, lo, hi):
            def step(t, _):
                for a in range(2):
                    i, j = at(a)
                    it = (i + t) % 4
                    for k in range(2):
                        p = pid(a, it, (j + (3 if k == 0 else 1)) % 4)
                        self.got(p, a)
                        self.piece(p, a, k, f_fwd2.at[self.n, a, it, k], nb2(a, 1 - 2 * k)).start()
                        self.share(p, a)
                return 0

            lax.fori_loop(lo, hi, step, 0)

        def second_far(self):
            def step(t, _):
                for a in range(2):
                    i, j = at(a)
                    p = pid(a, (i + t) % 4, (j + 2) % 4)
                    self.got_pieces(p, a)
                    self.share(p, a)
                return 0

            lax.fori_loop(0, 4, step, 0)

        def shared(self):
            def step(t, _):
                p = (m + t) % 16
                for a in range(2):
                    dst = self.buf.at[p, 1 - c, a]
                    rcopy(dst, dst, fs_send.at[self.n, p, a], fs_recv.at[self.n, p, a], sib).wait_recv()
                return 0

            lax.fori_loop(1, 16, step, 0)

        def sent(self):
            def step(i, _):
                for a in range(2):
                    p = pid(a, i, at(a)[1])
                    for k in range(2):
                        self.full(p, a, f_send2.at[self.n, a, i, k], f_recv.at[self.n, p, a, 0], sib).wait_send()
                        self.piece(p, a, k, f_fwd2.at[self.n, a, i, k], sib).wait_send()
                return 0

            lax.fori_loop(0, 4, step, 0)

            def step2(t, _):
                p = (m + t) % 16
                for a in range(2):
                    self.full(p, a, fs_send.at[self.n, p, a], fs_recv.at[self.n, p, a], sib).wait_send()
                return 0

            lax.fori_loop(1, 16, step2, 0)

    expand, reduce = Gather(0, eb), Gather(1, rb)
    for cp in own_e:
        cp.wait()
    expand.begin()
    expand.begin2()
    expand.first()
    expand.first_spread()
    expand.first_far()
    reduce.begin()
    reduce.begin2()
    for cp in own_s:
        cp.wait()
    r0 = lax.broadcasted_iota(jnp.int32, (16, 208), 0)
    j0 = lax.broadcasted_iota(jnp.int32, (16, 208), 1)
    u0 = j0 - 192
    fresh_ok = (j0 >= 192) & (u0 // 4 == r0 // 4) & (u0 % 4 <= r0 % 4)
    slot0 = j0 // 48
    pos0 = j0 % 48
    same = (j0 < 192) & (slot0 == r0 // 4)

    def make_bias(g, _):
        ln = jnp.zeros((16, 208), jnp.int32)
        for i in range(4):
            ln = jnp.where(slot0 == i, len_ref[g * 4 + i], ln)
        ok = fresh_ok | (same & (pos0 < ln))
        bias[g] = jnp.where(ok, 0.0, NEG)
        return 0

    lax.fori_loop(0, 16, make_bias, 0)

    ri = lax.broadcasted_iota(jnp.int32, (128, 128), 0)
    ci = lax.broadcasted_iota(jnp.int32, (128, 128), 1)

    def owners(k, carry):
        a, b = carry
        o = own_ref[k]
        return jnp.where(ri // 4 == k, o, a), jnp.where(ci // 4 == k, o, b)

    zero = jnp.zeros((128, 128), jnp.int32)
    own_rows, own_cols = lax.fori_loop(0, 32, owners, (zero, zero))
    eq = own_rows == own_cols
    rank_row = jnp.sum(jnp.where(eq & (ri // 4 < ci // 4) & (ri % 4 == 0), 1.0, 0.0), axis=0, keepdims=True)
    rank_col = jnp.sum(jnp.where(eq & (ci // 4 < ri // 4) & (ci % 4 == 0), 1.0, 0.0), axis=1, keepdims=True)
    tgt_row = own_cols[0:1, :] * 16 + rank_row.astype(jnp.int32) * 4 + ci[0:1, :] % 4
    tgt_col = own_rows[:, 0:1] * 16 + rank_col.astype(jnp.int32) * 4 + ri[:, 0:1] % 4
    perm[...] = jnp.where(lax.broadcasted_iota(jnp.int32, (256, 128), 0) == tgt_row, 1.0, 0.0).astype(BF)
    perm_t[...] = jnp.where(lax.broadcasted_iota(jnp.int32, (128, 256), 1) == tgt_col, 1.0, 0.0).astype(BF)

    own_w.wait()
    own_weight(1 - c).wait_recv()
    wt = wown[...].reshape(896, 896)
    for k in (1, 2, 0):
        hcopy(k, steps[k]).wait_recv()
        pout[k] = dot(hin[k], wt).astype(BF)
        go(pcopy(k, steps[k]))
    own_h.wait()
    pacc[...] = dot(hid[...], wt)
    expand.second(0, 4)
    reduce.first()
    for k in range(3):
        pcopy(k, steps[k]).wait_recv()
    projected = pacc[...] + pin[0].astype(F32) + pin[1].astype(F32) + pin[2].astype(F32)
    projected = projected.astype(BF).astype(F32)
    scale = lax.rsqrt(jnp.mean(projected * projected, axis=-1, keepdims=True) + 1e-06)
    normed = (projected * scale * gain_ref[...].astype(F32).reshape(1, 896)).astype(BF)
    packed[...] = dot(perm[...], normed).astype(BF).reshape(16, 16, 896)

    def post(k, _):
        o = (m + k) % 16
        rcopy(packed.at[o], inb.at[m], a_send.at[o], a_recv.at[m], (s, o, d)).start()
        return 0

    lax.fori_loop(1, 16, post, 0)
    inb[m] = packed[m]

    expand.second_far()
    for cp in own_q + own_kv + [own_n]:
        cp.wait()

    def arrive(k, _):
        o = (m + k) % 16
        rcopy(packed.at[o], inb.at[o], a_send.at[o], a_recv.at[o], (s, o, d)).wait()
        return 0

    lax.fori_loop(1, 16, arrive, 0)
    reduce.first_spread()
    reduce.first_far()
    qkv[...] = dot(inb[...].reshape(256, 896), wqkv[...]).astype(BF).reshape(16, 16, 1280)
    kbuf[:, 192:208, :] = qkv[:, :, 768:1024]
    vbuf[:, 192:208, :] = qkv[:, :, 1024:1280]

    factor = 128 ** (-0.5)

    def give(h, g):
        return rcopy(outb.at[h, g], retb.at[h, m], r_send.at[h, g], r_recv.at[h, m], (s, g, d))

    for h in range(2):
        kcols = slice(h * 128, (h + 1) * 128)
        for q4 in range(4):
            group = range(q4 * 4, q4 * 4 + 4)
            sc = []
            for g in group:
                q = [qkv[g, :, (h * 3 + e) * 128 : (h * 3 + e + 1) * 128] for e in range(3)]
                sc.append(dot_t(jnp.concatenate(q, axis=0), kbuf[g, :, kcols]).reshape(3, 16, 208))
            sc = jnp.stack(sc) * factor + bias[q4 * 4 : q4 * 4 + 4][:, None]
            pr = jnp.exp(sc - jnp.max(sc, axis=-1, keepdims=True))
            inv = (1.0 / jnp.sum(pr, axis=-1, keepdims=True)).reshape(4, 48, 1)
            pr = pr.astype(BF).reshape(4, 48, 208)
            for gg, g in enumerate(group):
                o = (dot(pr[gg], vbuf[g, :, kcols]) * inv[gg]).astype(BF)
                for e in range(3):
                    outb[h, g, :, e * 128 : (e + 1) * 128] = o[e * 16 : (e + 1) * 16]

            def give4(g, _):
                @pl.when(g != m)
                def _():
                    give(h, g).start()

                return 0

            lax.fori_loop(q4 * 4, q4 * 4 + 4, give4, 0)
        retb[h, m] = outb[h, m]
    reduce.second(0, 1)
    swaps = []
    for h in range(2):

        def back(k, _):
            o = (m + k) % 16
            rcopy(outb.at[h, o], retb.at[h, o], r_send.at[h, o], r_recv.at[h, o], (s, o, d)).wait()
            return 0

        lax.fori_loop(1, 16, back, 0)
        mine[h] = dot(perm_t[...], retb[h].reshape(256, 384)).astype(BF)
        swaps.append(rcopy(mine.at[h], part.at[h], x_send.at[h], x_recv.at[h], zdev(4)))
        swaps[h].start()
        if h == 0:
            reduce.second(1, 4)

    expand.shared()

    for t in range(8):
        e = eb[2 * t : 2 * t + 2, :, :, :, 0:1024].reshape(256, 1024)
        hpre[t] = dot_t(noisy[...], e)

    reduce.second_far()
    swaps[0].wait()

    for t in range(8):
        e = eb[2 * t : 2 * t + 2, :, :, :, 1024:1408].reshape(256, 384)
        hpre[t] += dot_t(part[0], e)

    swaps[1].wait()

    for t in range(8):
        e = eb[2 * t : 2 * t + 2, :, :, :, 1408:EXP].reshape(256, 384)
        hact[t] = jax.nn.gelu(hpre[t] + dot_t(part[1], e)).astype(BF)

    reduce.shared()
    h = jnp.concatenate([hact[t] for t in range(8)], axis=1)
    for n in range(4):
        cols = slice(n * 256, (n + 1) * 256)
        r = rb[:, :, :, :, cols].reshape(2048, 256)
        out_ref[:, cols] = (noisy[:, cols].astype(F32) + 0.5 * dot(h, r)).astype(BF)

    for cp in sends:
        cp.wait_send()
    expand.sent()
    reduce.sent()


def shards(hidden, owner, w, gain, wq, wk, wv, cache, fill, noisy, fe, fr):
    any_ = pl.BlockSpec(memory_space=pl.ANY)
    vmem = pl.BlockSpec(memory_space=pltpu.VMEM)
    dma = pltpu.SemaphoreType.DMA
    return pl.pallas_call(
        kernel,
        out_shape=jax.ShapeDtypeStruct((128, 1024), BF),
        in_specs=[any_, any_, any_, vmem, any_, any_, any_, any_, any_, any_, any_, any_],
        out_specs=vmem,
        scratch_shapes=[
            pltpu.SMEM((32,), jnp.int32),
            pltpu.SMEM((64,), jnp.int32),
            pltpu.VMEM((128, 896), BF),
            pltpu.VMEM((3, 128, 896), BF),
            pltpu.VMEM((3, 128, 896), BF),
            pltpu.VMEM((3, 128, 896), BF),
            pltpu.VMEM((2, 448, 896), BF),
            pltpu.VMEM((896, 1280), BF),
            pltpu.VMEM((16, 208, 256), BF),
            pltpu.VMEM((16, 208, 256), BF),
            pltpu.VMEM((128, 1024), BF),
            pltpu.VMEM((16, 2, 2, 32, EXP), BF),
            pltpu.VMEM((16, 2, 2, 32, 1024), BF),
            pltpu.VMEM((16, 16, 208), F32),
            pltpu.VMEM((256, 128), BF),
            pltpu.VMEM((128, 256), BF),
            pltpu.VMEM((128, 896), F32),
            pltpu.VMEM((16, 16, 896), BF),
            pltpu.VMEM((16, 16, 896), BF),
            pltpu.VMEM((16, 16, 1280), BF),
            pltpu.VMEM((2, 16, 16, 384), BF),
            pltpu.VMEM((2, 16, 16, 384), BF),
            pltpu.VMEM((2, 128, 384), BF),
            pltpu.VMEM((2, 128, 384), BF),
            pltpu.VMEM((8, 128, 256), F32),
            pltpu.VMEM((8, 128, 256), BF),
            dma((32,)),
            dma((1,)),
            dma((1,)),
            dma((3,)),
            dma((3,)),
            dma((3,)),
            dma((3,)),
            dma((2, 2, 2)),
            dma((2, 2, 4, 2)),
            dma((2, 2, 2)),
            dma((2, 2, 4, 2)),
            dma((2, 16, 2, 2)),
            dma((2, 16, 2)),
            dma((2, 16, 2)),
            dma((16,)),
            dma((16,)),
            dma((2, 16)),
            dma((2, 16)),
            dma((2,)),
            dma((2,)),
        ],
        compiler_params=pltpu.CompilerParams(
            collective_id=0, has_side_effects=True, vmem_limit_bytes=63 * 2**20
        ),
        name="talker_flow",
    )(
        hidden, owner, w, gain, wq, wk, wv, cache.reshape(16, 4, 2, 48, 256), fill, noisy, fe, fr,
    )


def solution(mesh):
    placed = (
        P(("segment", "mp", "dp"), None),
        P(("segment", "mp", "dp")),
        P("dp", None),
        P(),
        P(),
        P(),
        P(),
        P(("segment", "mp", "dp"), None, None, None),
        P(("segment", "mp", "dp")),
        P(("segment", "mp", "dp"), None),
        P("mp", None),
        P("mp", None),
    )
    return jax.shard_map(
        shards,
        mesh=mesh,
        in_specs=placed,
        out_specs=P(("segment", "mp", "dp"), None),
        check_vma=False,
    )
```

time: 76 us -> 70.6 us (0.929)
  the two profiles are of different devices: /device:TPU:16 before, /device:TPU:1 now
where the time goes in v3:
time: 70.6 us; the launch traced here: 70.2 us
  Pallas kernels  68.5 us (97%)
  local copies, waits for them, and re-layouts  1.67 us (2%)
    pallas_call x1, Pallas kernels, shards(): pl.pallas_call(kernel, out_shape=jax.ShapeDtypeStruct((128, 1024), BF), i...  68.5 us
    unnamed x1, local copies, waits for them, and re-layouts  1.67 us

profile of v3, /device:TPU:1, one launch (start us, length us, event | category | flops | bytes accessed | tf_op | source)
XLA Modules:
  0.0 70.2 jit_solution(16677905446466565386)
XLA Ops:
  0.0 68.5 %talker_flow.1 = bf16[128,1024]{1,0:T(8,128)(2,1)} custom-call(bf16[128,3584]{1,0:T(8,128)(2,1)} %hid_ref.1, s32[32]{0:T(128)} %own_hbm.1, bf16[448,896]{1,0:T(8,128)(2,1)} %w_ref.1, bf16[896]{0:T(1024)(128)(2,1)} %gain_ref.1, bf16[896,768]{1,0:T(8,128)(2,1)} %wq_ref.1, bf16[896,256]{1,0:T(8,128)(2,1)} %wk_ref.1, bf16[896,256]{1,0:T(8,128)(2,1)} %wv_ref.1, ...), custom_call_target="tpu_custom_call" | custom-call | tf_op jit(solution)/shard_map/talker_flow/pallas_call | solution.py:414
  68.5 1.7 %copy.14 = bf16[128,1024]{1,0:T(8,128)(2,1)} copy(bf16[128,1024]{1,0:T(8,128)(2,1)} %talker_flow.1) | data formatting | bytes 524288

commit v4 on v3

--- a/solution.py
+++ b/solution.py
@@ -23,7 +23,7 @@
 def kernel(
     hid_ref, own_hbm, w_ref, gain_ref, wq_ref, wk_ref, wv_ref, kv_ref, len_hbm, noisy_ref, fe_ref, fr_ref,
     out_ref,
-    own_ref, len_ref, hid, hin, pout, pin, wown, wqkv, kbuf, vbuf, noisy, eb, rb, bias, perm, perm_t, pacc, packed, inb, qkv, outb, retb, mine, part, hpre, hact,
+    own_ref, len_ref, hid, hin, pout0, pout1, pin0, pin1, wown, wqkv, kbuf, vbuf, noisy, eb, rb, bias, perm, perm_t, pacc, packed0, packed1, inb0, inb1, qkv, outb, retb, mine, part, hpre, hact,
     lsem, w_send, w_recv, h_send, h_recv, p_send, p_recv, f_send1, f_send2, f_fwd1, f_fwd2, f_recv, fs_send, fs_recv,
     a_send, a_recv, r_send, r_recv, x_send, x_recv,
 ):
@@ -94,14 +94,16 @@
         sends.append(cp)
 
     two = 2 - 4 * c
-    steps = (two, 1, -1)
+    steps = (1, -1, two)
 
     def hcopy(k, dz):
         cols = pl.ds(pl.multiple_of((zl + dz + 4) % 4 * 896, 128), 896)
         return rcopy(hid_ref.at[:, cols], hin.at[k], h_send.at[k], h_recv.at[k], zdev(dz))
 
-    def pcopy(k, dz):
-        return rcopy(pout.at[k], pin.at[k], p_send.at[k], p_recv.at[k], zdev(-dz))
+    halves = ((pout0, pin0, packed0, inb0, slice(0, 512)), (pout1, pin1, packed1, inb1, slice(512, 896)))
+
+    def pcopy(n, k, dz):
+        return rcopy(halves[n][0].at[k], halves[n][1].at[k], p_send.at[n, k], p_recv.at[n, k], zdev(-dz))
 
     def own_weight(cc):
         return rcopy(w_ref, wown.at[cc], w_send.at[0], w_recv.at[0], sib)
@@ -244,9 +246,28 @@
     expand.begin2()
     expand.first()
     expand.first_spread()
-    expand.first_far()
     reduce.begin()
     reduce.begin2()
+    own_w.wait()
+    own_weight(1 - c).wait_recv()
+    wt = wown[...].reshape(896, 896)
+
+    def partial(n, k):
+        pout, cols = halves[n][0], halves[n][4]
+        pout[k] = dot(hin[k], wt[:, cols]).astype(BF)
+        go(pcopy(n, k, steps[k]))
+
+    for k in range(2):
+        hcopy(k, steps[k]).wait_recv()
+        partial(0, k)
+    expand.first_far()
+    hcopy(2, steps[2]).wait_recv()
+    partial(0, 2)
+    for k in range(3):
+        partial(1, k)
+    own_h.wait()
+    pacc[...] = dot(hid[...], wt)
+
     for cp in own_s:
         cp.wait()
     r0 = lax.broadcasted_iota(jnp.int32, (16, 208), 0)
@@ -285,46 +306,43 @@
     perm[...] = jnp.where(lax.broadcasted_iota(jnp.int32, (256, 128), 0) == tgt_row, 1.0, 0.0).astype(BF)
     perm_t[...] = jnp.where(lax.broadcasted_iota(jnp.int32, (128, 256), 1) == tgt_col, 1.0, 0.0).astype(BF)
 
-    own_w.wait()
-    own_weight(1 - c).wait_recv()
-    wt = wown[...].reshape(896, 896)
-    for k in (1, 2, 0):
-        hcopy(k, steps[k]).wait_recv()
-        pout[k] = dot(hin[k], wt).astype(BF)
-        go(pcopy(k, steps[k]))
-    own_h.wait()
-    pacc[...] = dot(hid[...], wt)
     expand.second(0, 4)
     reduce.first()
-    for k in range(3):
-        pcopy(k, steps[k]).wait_recv()
-    projected = pacc[...] + pin[0].astype(F32) + pin[1].astype(F32) + pin[2].astype(F32)
-    projected = projected.astype(BF).astype(F32)
-    scale = lax.rsqrt(jnp.mean(projected * projected, axis=-1, keepdims=True) + 1e-06)
-    normed = (projected * scale * gain_ref[...].astype(F32).reshape(1, 896)).astype(BF)
-    packed[...] = dot(perm[...], normed).astype(BF).reshape(16, 16, 896)
-
-    def post(k, _):
-        o = (m + k) % 16
-        rcopy(packed.at[o], inb.at[m], a_send.at[o], a_recv.at[m], (s, o, d)).start()
-        return 0
-
-    lax.fori_loop(1, 16, post, 0)
-    inb[m] = packed[m]
-
-    expand.second_far()
+
+    for n in range(2):
+        _, pin, packed, inb, cols = halves[n]
+        for k in range(3):
+            pcopy(n, k, steps[k]).wait_recv()
+        projected = pacc[:, cols] + pin[0].astype(F32) + pin[1].astype(F32) + pin[2].astype(F32)
+        packed[...] = dot(perm[...], projected.astype(BF)).astype(BF).reshape(16, 16, -1)
+
+        def post(k, _):
+            o = (m + k) % 16
+            rcopy(packed.at[o], inb.at[m], a_send.at[n, o], a_recv.at[n, m], (s, o, d)).start()
+            return 0
+
+        lax.fori_loop(1, 16, post, 0)
+        inb[m] = packed[m]
+
     for cp in own_q + own_kv + [own_n]:
         cp.wait()
 
-    def arrive(k, _):
-        o = (m + k) % 16
-        rcopy(packed.at[o], inb.at[o], a_send.at[o], a_recv.at[o], (s, o, d)).wait()
-        return 0
-
-    lax.fori_loop(1, 16, arrive, 0)
+    for n in range(2):
+        _, _, packed, inb, _ = halves[n]
+
+        def arrive(k, _):
+            o = (m + k) % 16
+            rcopy(packed.at[o], inb.at[o], a_send.at[n, o], a_recv.at[n, o], (s, o, d)).wait()
+            return 0
+
+        lax.fori_loop(1, 16, arrive, 0)
+    expand.second_far()
     reduce.first_spread()
     reduce.first_far()
-    qkv[...] = dot(inb[...].reshape(256, 896), wqkv[...]).astype(BF).reshape(16, 16, 1280)
+    rows = jnp.concatenate([inb0[...].reshape(256, 512), inb1[...].reshape(256, 384)], axis=1).astype(F32)
+    scale = lax.rsqrt(jnp.mean(rows * rows, axis=-1, keepdims=True) + 1e-06)
+    normed = (rows * scale * gain_ref[...].astype(F32).reshape(1, 896)).astype(BF)
+    qkv[...] = dot(normed, wqkv[...]).astype(BF).reshape(16, 16, 1280)
     kbuf[:, 192:208, :] = qkv[:, :, 768:1024]
     vbuf[:, 192:208, :] = qkv[:, :, 1024:1280]
 
@@ -421,8 +439,10 @@
             pltpu.SMEM((64,), jnp.int32),
             pltpu.VMEM((128, 896), BF),
             pltpu.VMEM((3, 128, 896), BF),
-            pltpu.VMEM((3, 128, 896), BF),
-            pltpu.VMEM((3, 128, 896), BF),
+            pltpu.VMEM((3, 128, 512), BF),
+            pltpu.VMEM((3, 128, 384), BF),
+            pltpu.VMEM((3, 128, 512), BF),
+            pltpu.VMEM((3, 128, 384), BF),
             pltpu.VMEM((2, 448, 896), BF),
             pltpu.VMEM((896, 1280), BF),
             pltpu.VMEM((16, 208, 256), BF),
@@ -434,8 +454,10 @@
             pltpu.VMEM((256, 128), BF),
             pltpu.VMEM((128, 256), BF),
             pltpu.VMEM((128, 896), F32),
-            pltpu.VMEM((16, 16, 896), BF),
-            pltpu.VMEM((16, 16, 896), BF),
+            pltpu.VMEM((16, 16, 512), BF),
+            pltpu.VMEM((16, 16, 384), BF),
+            pltpu.VMEM((16, 16, 512), BF),
+            pltpu.VMEM((16, 16, 384), BF),
             pltpu.VMEM((16, 16, 1280), BF),
             pltpu.VMEM((2, 16, 16, 384), BF),
             pltpu.VMEM((2, 16, 16, 384), BF),
@@ -448,8 +470,8 @@
             dma((1,)),
             dma((3,)),
             dma((3,)),
-            dma((3,)),
-            dma((3,)),
+            dma((2, 3)),
+            dma((2, 3)),
             dma((2, 2, 2)),
             dma((2, 2, 4, 2)),
             dma((2, 2, 2)),
@@ -457,8 +479,8 @@
             dma((2, 16, 2, 2)),
             dma((2, 16, 2)),
             dma((2, 16, 2)),
-            dma((16,)),
-            dma((16,)),
+            dma((2, 16)),
+            dma((2, 16)),
             dma((2, 16)),
             dma((2, 16)),
             dma((2,)),

time: 70.6 us -> 68.2 us (0.966)
  the two profiles are of different devices: /device:TPU:1 before, /device:TPU:4 now
where the time goes in v4:
time: 68.2 us; the launch traced here: 68 us
  Pallas kernels  66.4 us (97%)
  local copies, waits for them, and re-layouts  1.67 us (2%)
    pallas_call x1, Pallas kernels, shards(): pl.pallas_call(kernel, out_shape=jax.ShapeDtypeStruct((128, 1024), BF), i...  66.4 us
    unnamed x1, local copies, waits for them, and re-layouts  1.67 us

profile of v4, /device:TPU:4, one launch (start us, length us, event | category | flops | bytes accessed | tf_op | source)
XLA Modules:
  0.0 68.0 jit_solution(10557461806392633478)
XLA Ops:
  0.0 66.4 %talker_flow.1 = bf16[128,1024]{1,0:T(8,128)(2,1)} custom-call(bf16[128,3584]{1,0:T(8,128)(2,1)} %hid_ref.1, s32[32]{0:T(128)} %own_hbm.1, bf16[448,896]{1,0:T(8,128)(2,1)} %w_ref.1, bf16[896]{0:T(1024)(128)(2,1)} %gain_ref.1, bf16[896,768]{1,0:T(8,128)(2,1)} %wq_ref.1, bf16[896,256]{1,0:T(8,128)(2,1)} %wk_ref.1, bf16[896,256]{1,0:T(8,128)(2,1)} %wv_ref.1, ...), custom_call_target="tpu_custom_call" | custom-call | tf_op jit(solution)/shard_map/talker_flow/pallas_call | solution.py:432
  66.4 1.7 %copy.14 = bf16[128,1024]{1,0:T(8,128)(2,1)} copy(bf16[128,1024]{1,0:T(8,128)(2,1)} %talker_flow.1) | data formatting | bytes 524288

commit v5 on v4

--- a/solution.py
+++ b/solution.py
@@ -74,17 +74,6 @@
             own_e.append(load(fr_ref.at[rows], rb.at[m, cc, a]))
     own_w = load(w_ref, wown.at[c])
     own_h = load(hid_ref.at[:, pl.ds(pl.multiple_of(zl * 896, 128), 896)], hid)
-    own_q = [
-        load(wq_ref, wqkv.at[:, pl.ds(0, 768)]),
-        load(wk_ref, wqkv.at[:, pl.ds(768, 256)]),
-        load(wv_ref, wqkv.at[:, pl.ds(1024, 256)]),
-    ]
-    own_n = load(noisy_ref, noisy)
-    own_kv = []
-    for i in range(4):
-        own_kv.append(load(kv_ref.at[:, i, 0], kbuf.at[:, pl.ds(i * 48, 48)]))
-        own_kv.append(load(kv_ref.at[:, i, 1], vbuf.at[:, pl.ds(i * 48, 48)]))
-
     pl.semaphore_wait(barrier, 21)
 
     sends = []
@@ -248,6 +237,17 @@
     expand.first_spread()
     reduce.begin()
     reduce.begin2()
+    own_q = [
+        load(wq_ref, wqkv.at[:, pl.ds(0, 768)]),
+        load(wk_ref, wqkv.at[:, pl.ds(768, 256)]),
+        load(wv_ref, wqkv.at[:, pl.ds(1024, 256)]),
+    ]
+    own_n = load(noisy_ref, noisy)
+    own_kv = []
+    for i in range(4):
+        own_kv.append(load(kv_ref.at[:, i, 0], kbuf.at[:, pl.ds(i * 48, 48)]))
+        own_kv.append(load(kv_ref.at[:, i, 1], vbuf.at[:, pl.ds(i * 48, 48)]))
+
     own_w.wait()
     own_weight(1 - c).wait_recv()
     wt = wown[...].reshape(896, 896)
@@ -324,11 +324,16 @@
         lax.fori_loop(1, 16, post, 0)
         inb[m] = packed[m]
 
+    expand.second_far()
+    reduce.first_spread()
+    reduce.first_far()
     for cp in own_q + own_kv + [own_n]:
         cp.wait()
 
+    gain = gain_ref[...].astype(F32).reshape(1, 896)
+    acc, square = 0.0, 0.0
     for n in range(2):
-        _, _, packed, inb, _ = halves[n]
+        _, _, packed, inb, cols = halves[n]
 
         def arrive(k, _):
             o = (m + k) % 16
@@ -336,13 +341,11 @@
             return 0
 
         lax.fori_loop(1, 16, arrive, 0)
-    expand.second_far()
-    reduce.first_spread()
-    reduce.first_far()
-    rows = jnp.concatenate([inb0[...].reshape(256, 512), inb1[...].reshape(256, 384)], axis=1).astype(F32)
-    scale = lax.rsqrt(jnp.mean(rows * rows, axis=-1, keepdims=True) + 1e-06)
-    normed = (rows * scale * gain_ref[...].astype(F32).reshape(1, 896)).astype(BF)
-    qkv[...] = dot(normed, wqkv[...]).astype(BF).reshape(16, 16, 1280)
+        rows = inb[...].reshape(256, -1).astype(F32)
+        square += jnp.sum(rows * rows, axis=-1, keepdims=True)
+        acc += dot((rows * gain[:, cols]).astype(BF), wqkv[cols, :])
+    scale = lax.rsqrt(square * (1 / 896) + 1e-06)
+    qkv[...] = (acc * scale).astype(BF).reshape(16, 16, 1280)
     kbuf[:, 192:208, :] = qkv[:, :, 768:1024]
     vbuf[:, 192:208, :] = qkv[:, :, 1024:1280]
 
@@ -400,29 +403,28 @@
         hpre[t] = dot_t(noisy[...], e)
 
     reduce.second_far()
+    for cp in sends:
+        cp.wait_send()
+    expand.sent()
     swaps[0].wait()
 
     for t in range(8):
         e = eb[2 * t : 2 * t + 2, :, :, :, 1024:1408].reshape(256, 384)
         hpre[t] += dot_t(part[0], e)
 
+    reduce.shared()
+    reduce.sent()
     swaps[1].wait()
 
     for t in range(8):
         e = eb[2 * t : 2 * t + 2, :, :, :, 1408:EXP].reshape(256, 384)
         hact[t] = jax.nn.gelu(hpre[t] + dot_t(part[1], e)).astype(BF)
 
-    reduce.shared()
     h = jnp.concatenate([hact[t] for t in range(8)], axis=1)
     for n in range(4):
         cols = slice(n * 256, (n + 1) * 256)
         r = rb[:, :, :, :, cols].reshape(2048, 256)
         out_ref[:, cols] = (noisy[:, cols].astype(F32) + 0.5 * dot(h, r)).astype(BF)
-
-    for cp in sends:
-        cp.wait_send()
-    expand.sent()
-    reduce.sent()
 
 
 def shards(hidden, owner, w, gain, wq, wk, wv, cache, fill, noisy, fe, fr):

time: 68.2 us -> 64.9 us (0.952)
  the two profiles are of different devices: /device:TPU:4 before, /device:TPU:1 now
where the time goes in v5:
time: 64.9 us; the launch traced here: 64.8 us
  Pallas kernels  63.1 us (97%)
  local copies, waits for them, and re-layouts  1.67 us (3%)
    pallas_call x1, Pallas kernels, shards(): pl.pallas_call(kernel, out_shape=jax.ShapeDtypeStruct((128, 1024), BF), i...  63.1 us
    unnamed x1, local copies, waits for them, and re-layouts  1.67 us

profile of v5, /device:TPU:1, one launch (start us, length us, event | category | flops | bytes accessed | tf_op | source)
XLA Modules:
  0.0 64.8 jit_solution(5125733203401537461)
XLA Ops:
  0.0 63.1 %talker_flow.1 = bf16[128,1024]{1,0:T(8,128)(2,1)} custom-call(bf16[128,3584]{1,0:T(8,128)(2,1)} %hid_ref.1, s32[32]{0:T(128)} %own_hbm.1, bf16[448,896]{1,0:T(8,128)(2,1)} %w_ref.1, bf16[896]{0:T(1024)(128)(2,1)} %gain_ref.1, bf16[896,768]{1,0:T(8,128)(2,1)} %wq_ref.1, bf16[896,256]{1,0:T(8,128)(2,1)} %wk_ref.1, bf16[896,256]{1,0:T(8,128)(2,1)} %wv_ref.1, ...), custom_call_target="tpu_custom_call" | custom-call | tf_op jit(solution)/shard_map/talker_flow/pallas_call | solution.py:434
  63.1 1.7 %copy.14 = bf16[128,1024]{1,0:T(8,128)(2,1)} copy(bf16[128,1024]{1,0:T(8,128)(2,1)} %talker_flow.1) | data formatting | bytes 524288

commit v6 on v5

--- a/solution.py
+++ b/solution.py
@@ -23,9 +23,9 @@
 def kernel(
     hid_ref, own_hbm, w_ref, gain_ref, wq_ref, wk_ref, wv_ref, kv_ref, len_hbm, noisy_ref, fe_ref, fr_ref,
     out_ref,
-    own_ref, len_ref, hid, hin, pout0, pout1, pin0, pin1, wown, wqkv, kbuf, vbuf, noisy, eb, rb, bias, perm, perm_t, pacc, packed0, packed1, inb0, inb1, qkv, outb, retb, mine, part, hpre, hact,
+    own_ref, len_ref, hid, hin, pout0, pout1, pin0, pin1, wown, wqkv, kbuf, vbuf, noisy, eb, rb, bias, perm, perm_t, pacc, packed0, packed1, inb0, inb1, qkv, outb, retb, mine, part, hpre, hact, obuf,
     lsem, w_send, w_recv, h_send, h_recv, p_send, p_recv, f_send1, f_send2, f_fwd1, f_fwd2, f_recv, fs_send, fs_recv,
-    a_send, a_recv, r_send, r_recv, x_send, x_recv,
+    a_send, a_recv, r_send, r_recv, x_send, x_recv, o_sem,
 ):
     s = lax.axis_index("segment")
     m = lax.axis_index("mp")
@@ -421,10 +421,16 @@
         hact[t] = jax.nn.gelu(hpre[t] + dot_t(part[1], e)).astype(BF)
 
     h = jnp.concatenate([hact[t] for t in range(8)], axis=1)
+    outs = []
     for n in range(4):
         cols = slice(n * 256, (n + 1) * 256)
         r = rb[:, :, :, :, cols].reshape(2048, 256)
-        out_ref[:, cols] = (noisy[:, cols].astype(F32) + 0.5 * dot(h, r)).astype(BF)
+        obuf[:, cols] = (noisy[:, cols].astype(F32) + 0.5 * dot(h, r)).astype(BF)
+        done = pltpu.make_async_copy(obuf.at[:, pl.ds(n * 256, 256)], out_ref.at[:, pl.ds(n * 256, 256)], o_sem.at[n])
+        done.start()
+        outs.append(done)
+    for done in outs:
+        done.wait()
 
 
 def shards(hidden, owner, w, gain, wq, wk, wv, cache, fill, noisy, fe, fr):
@@ -435,7 +441,7 @@
         kernel,
         out_shape=jax.ShapeDtypeStruct((128, 1024), BF),
         in_specs=[any_, any_, any_, vmem, any_, any_, any_, any_, any_, any_, any_, any_],
-        out_specs=vmem,
+        out_specs=any_,
         scratch_shapes=[
             pltpu.SMEM((32,), jnp.int32),
             pltpu.SMEM((64,), jnp.int32),
@@ -467,6 +473,7 @@
             pltpu.VMEM((2, 128, 384), BF),
             pltpu.VMEM((8, 128, 256), F32),
             pltpu.VMEM((8, 128, 256), BF),
+            pltpu.VMEM((128, 1024), BF),
             dma((32,)),
             dma((1,)),
             dma((1,)),
@@ -487,6 +494,7 @@
             dma((2, 16)),
             dma((2,)),
             dma((2,)),
+            dma((4,)),
         ],
         compiler_params=pltpu.CompilerParams(
             collective_id=0, has_side_effects=True, vmem_limit_bytes=63 * 2**20

time: 64.9 us -> 64.9 us (level)
  no operation moved by 1% of the time
where the time goes in v6:
time: 64.9 us; the launch traced here: 64.8 us
  Pallas kernels  63.1 us (97%)
  local copies, waits for them, and re-layouts  1.67 us (3%)
    pallas_call x1, Pallas kernels, shards(): pl.pallas_call(kernel, out_shape=jax.ShapeDtypeStruct((128, 1024), BF), i...  63.1 us
    unnamed x1, local copies, waits for them, and re-layouts  1.67 us

profile of v6, /device:TPU:1, one launch (start us, length us, event | category | flops | bytes accessed | tf_op | source)
XLA Modules:
  0.0 64.8 jit_solution(15412362263874519066)
XLA Ops:
  0.0 63.1 %talker_flow.1 = bf16[128,1024]{1,0:T(8,128)(2,1)} custom-call(bf16[128,3584]{1,0:T(8,128)(2,1)} %hid_ref.1, s32[32]{0:T(128)} %own_hbm.1, bf16[448,896]{1,0:T(8,128)(2,1)} %w_ref.1, bf16[896]{0:T(1024)(128)(2,1)} %gain_ref.1, bf16[896,768]{1,0:T(8,128)(2,1)} %wq_ref.1, bf16[896,256]{1,0:T(8,128)(2,1)} %wk_ref.1, bf16[896,256]{1,0:T(8,128)(2,1)} %wv_ref.1, ...), custom_call_target="tpu_custom_call" | custom-call | tf_op jit(solution)/shard_map/talker_flow/pallas_call | solution.py:440
  63.1 1.7 %copy.14 = bf16[128,1024]{1,0:T(8,128)(2,1)} copy(bf16[128,1024]{1,0:T(8,128)(2,1)} %talker_flow.1) | data formatting | bytes 524288
